TPU v7x, 512 devices: a whole 4x4x16 slice. The times are simulated.
512 devices in a mesh: row: 32 (over z_hi, x, core), col: 16 (over y, z_lo).
Axes of the slice: x: 4, y: 4, z: 16 (z_hi: 4, z_lo: 4; z = z_hi * 4 + z_lo), core: 2. Of those that a mesh axis runs over, the one named last changes fastest.
Arguments:
- pair: bfloat16 [1024, 1024, 128], P('row', 'col'), may hold values from -110 to 110
- mask: int32 [1024], replicated, may hold values 0 or 1
- w_tri_in: bfloat16 [128, 640], replicated, may hold values from -0.5 to 0.5
- w_tri_out: bfloat16 [128, 128], replicated, may hold values from -0.5 to 0.5
- w_bias: bfloat16 [128, 64], replicated, may hold values from -0.5 to 0.5
- single: bfloat16 [16, 1024, 768], P(None, 'row'), may hold values from -6 to 6
- w_attn: bfloat16 [768, 16, 192], P(None, 'col'), may hold values from -2 to 2
- w_out: bfloat16 [768, 768], P('col'), may hold values from -0.21875 to 0.21875
Outputs:
- new_pair: bfloat16 [1024, 1024, 128], P('row', 'col')
- biases: bfloat16 [4, 16, 1024, 1024], P(None, 'col', 'row')
- attended: bfloat16 [16, 1024, 768], P('col', 'row')
All inputs are finite; a program needn't handle non-finite values.
Results may differ from a plain program's by a relative error of at most 0.025.
The roundings to bfloat16 on the way count: a program that leaves them out, or rounds other values in their place, can miss the bound.
Values may be sent and summed in bfloat16 or wider, within the bound.
A program may use at most 64 MiB of HBM per device.

v0:
```python
import jax
import jax.numpy as jnp
from jax import lax
from jax.sharding import PartitionSpec as P

HEADS = 16
HEAD_DIM = 48
LAYERS = 4


def layer_norm(value, axis):
    mean = jnp.mean(value, axis=axis, keepdims=True)
    centred = value - mean
    var = jnp.mean(centred * centred, axis=axis, keepdims=True)
    return centred * lax.rsqrt(var + 1e-05)


def per_device(pair, mask, w_tri_in, w_tri_out, w_bias, single, w_attn, w_out):
    rows_dev, cols_dev, chans = pair.shape
    row_index = lax.axis_index("row")
    col_index = lax.axis_index("col")
    maskf = mask.astype(jnp.float32)
    row_mask = lax.dynamic_slice_in_dim(maskf, row_index * rows_dev, rows_dev)
    col_mask = lax.dynamic_slice_in_dim(maskf, col_index * cols_dev, cols_dev)
    pair_mask = row_mask[:, None] * col_mask[None, :]
    pair_f = pair.astype(jnp.float32)
    normed = layer_norm(pair_f, 2).astype(jnp.bfloat16)
    leading = jnp.einsum(
        "ijc,cd->dij", normed, w_tri_in[:, : 4 * chans], preferred_element_type=jnp.float32
    )
    left = (jax.nn.sigmoid(leading[chans : 2 * chans]) * leading[:chans] * pair_mask).astype(
        jnp.bfloat16
    )
    right = (
        jax.nn.sigmoid(leading[3 * chans :]) * leading[2 * chans : 3 * chans] * pair_mask
    ).astype(jnp.bfloat16)
    gate = jax.nn.sigmoid(
        jnp.einsum(
            "ijc,cd->ijd", normed, w_tri_in[:, 4 * chans :], preferred_element_type=jnp.float32
        )
    )
    left_full, right_full = (
        lax.all_to_all(left, "row", split_axis=0, concat_axis=1, tiled=True),
        lax.all_to_all(right, "row", split_axis=0, concat_axis=1, tiled=True),
    )
    summed = jnp.einsum(
        "cki,ckj->cij",
        lax.all_gather(left_full, "col", axis=2, tiled=True),
        right_full,
        preferred_element_type=jnp.float32,
    )
    tri_tile = lax.all_to_all(
        summed.astype(jnp.bfloat16), "row", split_axis=1, concat_axis=0, tiled=True
    )
    tnorm = layer_norm(tri_tile.astype(jnp.float32), 0).astype(jnp.bfloat16)
    update = jnp.einsum("cij,cd->ijd", tnorm, w_tri_out, preferred_element_type=jnp.float32)
    new_pair = (pair_f + gate * update).astype(jnp.bfloat16)
    pnorm = layer_norm(new_pair.astype(jnp.float32), 2).astype(jnp.bfloat16)
    bias_tile = jnp.einsum("ijc,cl->lij", pnorm, w_bias, preferred_element_type=jnp.float32).astype(
        jnp.bfloat16
    )
    bias_tile = bias_tile.reshape(LAYERS, HEADS, rows_dev, cols_dev)
    biases = lax.all_to_all(bias_tile, "col", split_axis=1, concat_axis=3, tiled=True)
    xn = layer_norm(single.astype(jnp.float32), 2).astype(jnp.bfloat16)
    projected = jnp.einsum("srd,dhe->shre", xn, w_attn, preferred_element_type=jnp.float32)
    query = projected[..., :HEAD_DIM].astype(jnp.bfloat16)
    keyval = projected[..., HEAD_DIM : 3 * HEAD_DIM].astype(jnp.bfloat16)
    agate = jax.nn.sigmoid(projected[..., 3 * HEAD_DIM :])
    keyval_all = lax.all_gather(keyval, "row", axis=2, tiled=True)
    score = jnp.einsum(
        "shqe,shke->shqk", query, keyval_all[..., :HEAD_DIM], preferred_element_type=jnp.float32
    )
    score = score * HEAD_DIM ** (-0.5) + biases[0].astype(jnp.float32)[None]
    score = jnp.where((mask > 0)[None, None, None, :], score, -1000000000.0)
    peak = jnp.max(score, axis=3, keepdims=True)
    expo = jnp.exp(score - peak)
    probs = (expo / jnp.sum(expo, axis=3, keepdims=True)).astype(jnp.bfloat16)
    context = jnp.einsum(
        "shqk,shke->shqe", probs, keyval_all[..., HEAD_DIM:], preferred_element_type=jnp.float32
    )
    gated = (agate * context).astype(jnp.bfloat16)
    heads_dev = gated.shape[1]
    out_local = w_out.reshape(heads_dev, HEAD_DIM, w_out.shape[1])
    attended = lax.psum_scatter(
        jnp.einsum("shqe,hed->sqd", gated, out_local, preferred_element_type=jnp.float32).astype(
            jnp.bfloat16
        ),
        "col",
        scatter_dimension=0,
        tiled=True,
    )
    return (new_pair, biases, attended)


def solution(mesh):
    placed = (
        P("row", "col", None),
        P(),
        P(),
        P(),
        P(),
        P(None, "row", None),
        P(None, "col", None),
        P("col", None),
    )
    return jax.shard_map(
        per_device,
        mesh=mesh,
        in_specs=placed,
        out_specs=(P("row", "col", None), P(None, "col", "row", None), P("col", "row", None)),
        check_vma=False,
    )
```

profile of v0, /device:TPU:6, one launch (start us, length us, event | category | flops | bytes accessed | tf_op | source)
XLA Modules:
  0.0 502.6 jit_solution(16179217679759600691)
XLA Ops:
  8.1 1.4 convert_reduce_fusion.1
  9.5 1.7 fusion.23
  11.3 2.0 convolution_bitcast_fusion
  13.9 1.6 copy.46
  16.2 45.4 %all_to_all.63 = bf16[32,2,4096]{2,1,0:T(2,128)(2,1)S(1)} all-to-all(bf16[32,2,4096]{2,1,0:T(2,128)(2,1)S(1)} %reshape.163), channel_id=1, replica_groups=mesh['row'=32,'col'=16] {'row'}, dimensions={0} | all-to-all | bytes 1048576 | tf_op jit(solution)/shard_map/all_to_all | solution.py:43
  62.4 1.1 copy.48
  63.6 1.6 copy.49
  65.2 1.6 reshape.165
  66.8 10.8 %all-to-all-start.1 = ((bf16[32,2,4096]{2,1,0:T(2,128)(2,1)}), bf16[32,2,4096]{2,1,0:T(2,128)(2,1)S(1)}, u32[]{:S(2)}, u32[]{:S(2)}) async-start(bf16[32,2,4096]{2,1,0:T(2,128)(2,1)} %reshape.165), calls=%async_computation.1 | async-start | bytes 1048576 | tf_op jit(solution)/shard_map/all_to_all | solution.py:44
  78.4 1.3 fusion.70
  80.4 30.6 %all-to-all-done.1 = bf16[32,2,4096]{2,1,0:T(2,128)(2,1)S(1)} async-done(((bf16[32,2,4096]{2,1,0:T(2,128)(2,1)}), bf16[32,2,4096]{2,1,0:T(2,128)(2,1)S(1)}, u32[]{:S(2)}, u32[]{:S(2)}) %all-to-all-start.1) | async-done | bytes 524320 | tf_op jit(solution)/shard_map/all_to_all | solution.py:44
  111.8 163.3 %all-gather.3.cloned.1.call-done = bf16[4,1024,1024]{1,2,0:T(8,128)(2,1)} async-done(((bf16[4,1024,64]{1,2,0:T(8,128)(2,1)}), bf16[4,1024,1024]{1,2,0:T(8,128)(2,1)}) %all-gather.3.cloned.1.call-update) | async-done | bytes 8388624 | tf_op jit(solution)/shard_map/all_gather | solution.py:48
  275.1 6.0 %convolution_convert_fusion.1 = bf16[4,1024,64]{1,2,0:T(8,128)(2,1)S(1)} fusion(bf16[4,1024,1024]{1,2,0:T(8,128)(2,1)} %all-gather.3.cloned.1.call-done, bf16[4,1024,64]{2,1,0:T(8,128)(2,1)S(1)} %bitcast.120), kind=kOutput, calls=%fused_computation.33 | convolution fusion | flops 537133056 | bytes 9437184 | tf_op jit(solution)/shard_map/cki,ckj->cij/dot_general | solution.py:46
  281.9 1.5 reshape.167
  283.4 14.2 %all-to-all-start.2 = ((bf16[32,2,4096]{2,1,0:T(2,128)(2,1)}), bf16[32,2,4096]{2,1,0:T(2,128)(2,1)S(1)}, u32[]{:S(2)}, u32[]{:S(2)}) async-start(bf16[32,2,4096]{2,1,0:T(2,128)(2,1)} %reshape.167), calls=%async_computation.2 | async-start | bytes 1048576 | tf_op jit(solution)/shard_map/all_to_all | solution.py:52
  297.6 1.5 fusion.12
  299.1 35.4 %all-to-all-done.2 = bf16[32,2,4096]{2,1,0:T(2,128)(2,1)S(1)} async-done(((bf16[32,2,4096]{2,1,0:T(2,128)(2,1)}), bf16[32,2,4096]{2,1,0:T(2,128)(2,1)S(1)}, u32[]{:S(2)}, u32[]{:S(2)}) %all-to-all-start.2) | async-done | bytes 524320 | tf_op jit(solution)/shard_map/all_to_all | solution.py:52
  339.8 1.1 reshape.169
  340.9 5.7 %all-to-all-start.3 = ((bf16[16,2,4096]{2,1,0:T(2,128)(2,1)}), bf16[16,2,4096]{2,1,0:T(2,128)(2,1)S(1)}, u32[]{:S(2)}, u32[]{:S(2)}) async-start(bf16[16,2,4096]{2,1,0:T(2,128)(2,1)} %reshape.169), calls=%async_computation.3 | async-start | bytes 524288 | tf_op jit(solution)/shard_map/all_to_all | solution.py:63
  346.9 22.5 %all-to-all-done.3 = bf16[16,2,4096]{2,1,0:T(2,128)(2,1)S(1)} async-done(((bf16[16,2,4096]{2,1,0:T(2,128)(2,1)}), bf16[16,2,4096]{2,1,0:T(2,128)(2,1)S(1)}, u32[]{:S(2)}, u32[]{:S(2)}) %all-to-all-start.3) | async-done | bytes 262176 | tf_op jit(solution)/shard_map/all_to_all | solution.py:63
  370.1 28.3 %all-gather.5.cloned.1.call-done = bf16[16,1,1024,96]{3,2,0,1:T(8,128)(2,1)} async-done(((bf16[16,1,32,96]{3,2,0,1:T(8,128)(2,1)}), bf16[16,1,1024,96]{3,2,0,1:T(8,128)(2,1)}) %all-gather.5.cloned.1.call-update) | async-done | bytes 3145744 | tf_op jit(solution)/shard_map/all_gather | solution.py:69
  398.4 5.1 %fusion.71 = (f32[16,32]{1,0:T(8,128)S(1)}, f32[16,32,1024]{2,1,0:T(8,128)}) fusion(f32[32,1024]{1,0:T(8,128)S(1)} %reshape.154, pred[1024]{0:T(1024)(128)(4,1)S(1)} %broadcast_compare_fusion, bf16[16,1,1024,96]{3,2,0,1:T(8,128)(2,1)} %all-gather.5.cloned.1.call-done, bf16[16,1,32,192]{3,2,0,1:T(8,128)(2,1)S(1)} %copy-done.5), kind=kOutput, calls=%fused_computation.104 | convolution fusion | flops 52954112 | bytes 5508096 | tf_op jit(solution)/shard_map/sub | solution.py:76
  403.6 5.6 %convolution_convert_fusion = bf16[16,32,768]{2,1,0:T(8,128)(2,1)} fusion(bf16[16,1,1024,96]{3,2,0,1:T(8,128)(2,1)} %all-gather.5.cloned.1.call-done, f32[16,32,1024]{2,1,0:T(8,128)} %get-tuple-element.18, f32[16,32]{1,0:T(8,128)S(1)} %get-tuple-element.17, f32[16,1,32,192]{3,2,0,1:T(8,128)S(1)} %copy-done.10, bf16[48,768]{1,0:T(8,128)(2,1)S(1)} %copy-done.8), kind=kOutput, calls=%fused_computation.24 | convolution fusion | flops 89645056 | bytes 6373376 | tf_op jit(solution)/shard_map/shqe,hed->sqd/dot_general | solution.py:85
  410.6 85.4 %reduce-scatter.2.cloned.1.call-done = bf16[1,32,768]{2,1,0:T(8,128)(2,1)} async-done(((bf16[16,32,768]{2,1,0:T(8,128)(2,1)}), bf16[1,32,768]{2,1,0:T(8,128)(2,1)}) %reduce-scatter.2.cloned.1.call-update) | async-done | bytes 49168 | tf_op jit(solution)/shard_map/reduce_scatter | solution.py:84
  (69 shorter events, 13.6 us)
Async XLA Ops:
  7.2 71.2 %copy-start = (bf16[768,1,192]{0,2,1:T(8,128)(2,1)S(1)}, bf16[768,1,192]{0,2,1:T(8,128)(2,1)}, u32[]{:S(2)}) copy-start(bf16[768,1,192]{0,2,1:T(8,128)(2,1)} %param.14) | copy-start | bytes 884740
  7.2 267.9 %all-gather.3.cloned.1.call-start = ((), (), s32[]{:S(2)}) async-start(), calls=%async_computation.5 | async-start | bytes 8912896 | tf_op jit(solution)/shard_map/all_gather | solution.py:48
  63.6 14.2 %copy-start.2 = (bf16[16,32,768]{2,1,0:T(8,128)(2,1)S(1)}, bf16[16,32,768]{2,1,0:T(8,128)(2,1)}, u32[]{:S(2)}) copy-start(bf16[16,32,768]{2,1,0:T(8,128)(2,1)} %param.13) | copy-start | bytes 2359300
  66.8 44.2 %all-to-all-start.1 = ((bf16[32,2,4096]{2,1,0:T(2,128)(2,1)}), bf16[32,2,4096]{2,1,0:T(2,128)(2,1)S(1)}, u32[]{:S(2)}, u32[]{:S(2)}) async-start(bf16[32,2,4096]{2,1,0:T(2,128)(2,1)} %reshape.165), calls=%async_computation.1 | async-start | bytes 1048576 | tf_op jit(solution)/shard_map/all_to_all | solution.py:44
  77.6 320.8 %all-gather.5.cloned.1.call-start = ((), (), s32[]{:S(2)}) async-start(), calls=%async_computation.6 | async-start | bytes 4325376 | tf_op jit(solution)/shard_map/all_gather | solution.py:69
  79.7 0.8 copy-start.4
  281.1 16.4 %copy-start.1 = (bf16[32,64,128]{2,1,0:T(8,128)(2,1)S(1)}, bf16[32,64,128]{2,1,0:T(8,128)(2,1)}, u32[]{:S(2)}) copy-start(bf16[32,64,128]{2,1,0:T(8,128)(2,1)} %param.8) | copy-start | bytes 1572868
  283.4 51.1 %all-to-all-start.2 = ((bf16[32,2,4096]{2,1,0:T(2,128)(2,1)}), bf16[32,2,4096]{2,1,0:T(2,128)(2,1)S(1)}, u32[]{:S(2)}, u32[]{:S(2)}) async-start(bf16[32,2,4096]{2,1,0:T(2,128)(2,1)} %reshape.167), calls=%async_computation.2 | async-start | bytes 1048576 | tf_op jit(solution)/shard_map/all_to_all | solution.py:52
  336.0 0.8 copy-start.6
  336.7 1.5 copy-start.9
  337.5 3.4 copy-start.3
  338.2 8.6 %copy-start.7 = (s32[1024]{0:T(1024)S(1)}, s32[1024]{0:T(1024)}, u32[]{:S(2)}) copy-start(s32[1024]{0:T(1024)} %param.9) | copy-start | bytes 12292
  339.8 58.7 %copy-start.5 = (bf16[16,1,32,192]{3,2,0,1:T(8,128)(2,1)S(1)}, bf16[16,1,32,192]{3,2,0,1:T(8,128)(2,1)}, u32[]{:S(2)}) copy-start(bf16[16,1,32,192]{3,2,0,1:T(8,128)(2,1)} %copy-done.4) | copy-start | bytes 589828
  340.9 28.5 %all-to-all-start.3 = ((bf16[16,2,4096]{2,1,0:T(2,128)(2,1)}), bf16[16,2,4096]{2,1,0:T(2,128)(2,1)S(1)}, u32[]{:S(2)}, u32[]{:S(2)}) async-start(bf16[16,2,4096]{2,1,0:T(2,128)(2,1)} %reshape.169), calls=%async_computation.3 | async-start | bytes 524288 | tf_op jit(solution)/shard_map/all_to_all | solution.py:63
  346.6 149.5 %reduce-scatter.2.cloned.1.call-start = ((), (), s32[]{:S(2)}) async-start(), calls=%async_computation.7 | async-start | bytes 835584 | tf_op jit(solution)/shard_map/reduce_scatter | solution.py:84
  370.1 33.5 %copy-start.8 = (bf16[48,768]{1,0:T(8,128)(2,1)S(1)}, bf16[48,768]{1,0:T(8,128)(2,1)}, u32[]{:S(2)}) copy-start(bf16[48,768]{1,0:T(8,128)(2,1)} %param.15) | copy-start | bytes 221188
  370.1 33.5 %copy-start.10 = (f32[16,1,32,192]{3,2,0,1:T(8,128)S(1)}, f32[16,1,32,192]{3,2,0,1:T(8,128)}, u32[]{:S(2)}) copy-start(f32[16,1,32,192]{3,2,0,1:T(8,128)} %get-tuple-element.16) | copy-start | bytes 1179652
Sparse Core Ops, SparseCore 0:
  63.7 211.3 all-gather.2
  278.1 120.2 all-gather.4
  409.3 86.6 reduce-scatter.1
where the time goes:
time: 503 us
  waiting for transfers between devices  366 us (73%)
  blocking collectives  45.4 us (9%)
  starting transfers between devices  31.1 us (6%)
  matrix products  23 us (5%)
  local copies, waits for them, and re-layouts  16.3 us (3%)
  between operations  14.2 us (3%)
  other arithmetic  6.87 us (1%)
    all_gather x1, waiting for transfers between devices, per_device(): lax.all_gather(left_full, 'col', axis=2, tiled=True)  163 us
    reduce_scatter x1, waiting for transfers between devices, per_device(): lax.psum_scatter(jnp.einsum('shqe,hed->sqd', gated, out_local, preferred_...  85.4 us
    all_to_all x1, blocking collectives, per_device(): lax.all_to_all(left, 'row', split_axis=0, concat_axis=1, tiled=True)  45.4 us
    all_to_all x1, waiting for transfers between devices, per_device(): lax.all_to_all(summed.astype(jnp.bfloat16), 'row', split_axis=1, concat_a...  35.4 us
    all_to_all x1, waiting for transfers between devices, per_device(): lax.all_to_all(right, 'row', split_axis=0, concat_axis=1, tiled=True)  30.6 us
    all_gather x1, waiting for transfers between devices, per_device(): keyval_all = lax.all_gather(keyval, 'row', axis=2, tiled=True)  28.3 us
    all_to_all x1, waiting for transfers between devices, per_device(): lax.all_to_all(bias_tile, 'col', split_axis=1, concat_axis=3, tiled=True)  22.5 us
    all_to_all x1, starting transfers between devices, per_device(): lax.all_to_all(summed.astype(jnp.bfloat16), 'row', split_axis=1, concat_a...  14.2 us
  transfers between devices with their start and end apart: 6, of which 6 were waited for; matrix products, arithmetic and copies ran while one was open for 5% of the time, Pallas kernels for 0%

commit v1 on v0

v1 whole, which is shorter than its diff:
```python
import jax
import jax.numpy as jnp
from jax import lax
from jax.experimental import pallas as pl
from jax.experimental.pallas import tpu as pltpu
from jax.sharding import Mesh
from jax.sharding import PartitionSpec as P

HEADS = 16
HEAD_DIM = 48
LAYERS = 4
ROW = ("z_hi", "x", "core")
COL = ("y", "z_lo")


def layer_norm(value, axis):
    mean = jnp.mean(value, axis=axis, keepdims=True)
    centred = value - mean
    var = jnp.mean(centred * centred, axis=axis, keepdims=True)
    return centred * lax.rsqrt(var + 1e-05)


def each(count, body):
    lax.fori_loop(0, count, lambda step, carry: (body(step), carry)[1], 0)


def wait_bytes(ref, sem):
    pltpu.make_async_copy(ref, ref, sem).wait()


def triangle_kernel(
    left_in, right_in, keyval_in, w_out_in,
    tri_out, keyval_out, w_out_all,
    left_x, right_x, left_z, right_z, left_all, right_own, sums, sums_x,
    send, recv, local,
):
    z_hi, z_lo = lax.axis_index("z_hi"), lax.axis_index("z_lo")
    x, core, y = lax.axis_index("x"), lax.axis_index("core"), lax.axis_index("y")
    z, xc = z_hi * 4 + z_lo, x * 2 + core
    head = y * 4 + z_lo

    def z_peer(step):
        peer = lax.rem(z + 1 + step, 16)
        return peer, {"z_hi": lax.div(peer, 4), "z_lo": lax.rem(peer, 4)}

    def xc_peer(step):
        peer = lax.rem(xc + 1 + step, 8)
        return peer, {"x": lax.div(peer, 2), "core": lax.rem(peer, 2)}

    def near(axis, place, step, size):
        return {axis: lax.rem(place + 1 + step, size)}

    barrier = pltpu.get_barrier_semaphore()

    def greet(peer):
        pl.semaphore_signal(barrier, inc=1, device_id=peer, device_id_type=pl.DeviceIdType.MESH)

    each(15, lambda step: greet(z_peer(step)[1]))
    each(7, lambda step: greet(xc_peer(step)[1]))
    each(3, lambda step: greet(near("y", y, step, 4)))
    pl.semaphore_wait(barrier, 25)

    def push(src, dst, slot, peer):
        pltpu.make_async_remote_copy(
            src_ref=src, dst_ref=dst, send_sem=send.at[slot], recv_sem=recv.at[slot],
            device_id=peer, device_id_type=pl.DeviceIdType.MESH,
        ).start()

    def keep(src, dst, slot):
        pltpu.make_async_copy(src, dst, local.at[slot]).start()

    def over_x(src, dst, slot):
        def body(step):
            peer, place = xc_peer(step)
            push(src.at[:, peer], dst.at[:, xc], slot, place)
        each(7, body)
        keep(src.at[:, xc], dst.at[:, xc], slot)

    def end_x(dst, slot):
        wait_bytes(dst.at[pl.ds(0, 14)], recv.at[slot])
        wait_bytes(dst.at[pl.ds(0, 2)], local.at[slot])

    def over_z(src, dst, slot):
        def body(step):
            peer, place = z_peer(step)
            push(src.at[peer], dst.at[z], slot, place)
        each(15, body)
        keep(src.at[z], dst.at[z], slot)

    def end_z(dst, slot):
        wait_bytes(dst.at[pl.ds(0, 15)], recv.at[slot])
        wait_bytes(dst.at[pl.ds(0, 1)], local.at[slot])

    over_x(left_in, left_x, 0)
    over_x(right_in, right_x, 1)
    half = w_out_in.at[:, pl.ds(pl.multiple_of(core * 384, 128), 384)]
    each(3, lambda step: push(half, w_out_all.at[core, head], 6, near("z_lo", z_lo, step, 4)))
    keep(half, w_out_all.at[core, head], 6)
    end_x(left_x, 0)
    over_z(left_x, left_z, 2)
    end_x(right_x, 1)
    over_z(right_x, right_z, 3)
    mine = keyval_out.at[z_hi * 4 + x, core]
    each(3, lambda step: push(keyval_in, mine, 9, near("z_hi", z_hi, step, 4)))
    keep(keyval_in, mine, 9)
    wait_bytes(w_out_all.at[0, pl.ds(0, 3)], recv.at[6])
    wait_bytes(w_out_all.at[0, pl.ds(0, 1)], local.at[6])
    quad = w_out_all.at[core, pl.ds(y * 4, 4)]
    each(3, lambda step: push(quad, quad, 7, near("y", y, step, 4)))

    def tiles(blocks, z_part, part):
        pieces = [blocks[z_part * 4 + lo, :, :, part * 64 : part * 64 + 64] for lo in range(4)]
        return jnp.concatenate(pieces, axis=-1).reshape(128, 256)

    end_z(left_z, 2)
    for z_part in range(4):
        for part in range(2):
            block = tiles(left_z, z_part, part)
            first = z_part * 256 + part * 128
            left_all[y, :, first : first + 128] = block.T
    own = left_all.at[y]
    each(3, lambda step: push(own, own, 5, near("y", y, step, 4)))
    end_z(right_z, 3)
    for z_part in range(4):
        for part in range(2):
            first = z_part * 256 + part * 128
            right_own[first : first + 128, :] = tiles(right_z, z_part, part)
    wait_bytes(left_all.at[pl.ds(0, 3)], recv.at[5])

    def contract(part):
        product = jnp.dot(left_all[part], right_own[...], preferred_element_type=jnp.float32)
        product = product.astype(jnp.bfloat16).reshape(8, 2, 16, 256)
        for lo in range(4):
            cut = slice(lo * 64, lo * 64 + 64)
            sums[part * 4 + lo] = jnp.concatenate(
                [product[:, 0, :, cut], product[:, 1, :, cut]], axis=-1
            )

    each(4, contract)
    over_x(sums, sums_x, 4)
    wait_bytes(keyval_out.at[pl.ds(0, 3), 0], recv.at[9])
    wait_bytes(keyval_out.at[pl.ds(0, 1), 0], local.at[9])
    end_x(sums_x, 4)
    over_z(sums_x, tri_out, 8)

    def spread(part):
        block = keyval_out.at[part * 4 + x, core]
        each(3, lambda step: push(block, block, 10, near("x", x, step, 4)))

    each(4, spread)
    wait_bytes(w_out_all.at[0, pl.ds(0, 12)], recv.at[7])
    other = {"core": 1 - core}
    push(w_out_all.at[core], w_out_all.at[core], 12, other)
    wait_bytes(keyval_out.at[pl.ds(0, 12), 0], recv.at[10])
    push(keyval_out.at[:, core], keyval_out.at[:, core], 11, other)
    end_z(tri_out, 8)
    wait_bytes(keyval_out.at[:, 0], recv.at[11])
    wait_bytes(w_out_all.at[0], recv.at[12])
    for slot in (0, 1, 4):
        wait_bytes(left_x.at[pl.ds(0, 14)], send.at[slot])
    for slot in (2, 3, 8):
        wait_bytes(left_z.at[pl.ds(0, 15)], send.at[slot])
    wait_bytes(left_all.at[pl.ds(0, 3)], send.at[5])
    wait_bytes(w_out_all.at[0, pl.ds(0, 3)], send.at[6])
    wait_bytes(w_out_all.at[0, pl.ds(0, 12)], send.at[7])
    wait_bytes(keyval_out.at[pl.ds(0, 3), 0], send.at[9])
    wait_bytes(keyval_out.at[pl.ds(0, 12), 0], send.at[10])
    wait_bytes(keyval_out.at[:, 0], send.at[11])
    wait_bytes(w_out_all.at[0], send.at[12])


def triangle(left, right, keyval, w_out):
    vmem = pl.BlockSpec(memory_space=pltpu.VMEM)
    hbm = pl.BlockSpec(memory_space=pl.ANY)
    blocks = pltpu.VMEM((16, 8, 16, 128), jnp.bfloat16)
    return pl.pallas_call(
        triangle_kernel,
        out_shape=(
            jax.ShapeDtypeStruct((16, 8, 16, 128), jnp.bfloat16),
            jax.ShapeDtypeStruct((16, 2, 4, 32, 384), jnp.bfloat16),
            jax.ShapeDtypeStruct((2, 16, 48, 384), jnp.bfloat16),
        ),
        in_specs=[vmem] * 4,
        out_specs=(vmem, vmem, vmem),
        scratch_shapes=[
            blocks, blocks, blocks, blocks,
            pltpu.VMEM((4, 256, 1024), jnp.bfloat16),
            pltpu.VMEM((1024, 256), jnp.bfloat16),
            blocks, blocks,
            pltpu.SemaphoreType.DMA((13,)),
            pltpu.SemaphoreType.DMA((13,)),
            pltpu.SemaphoreType.DMA((10,)),
        ],
        compiler_params=pltpu.CompilerParams(
            collective_id=0, has_side_effects=True, vmem_limit_bytes=40 * 1024 * 1024
        ),
        name="triangle",
    )(left, right, keyval, w_out)


def per_device(pair, mask, w_tri_in, w_tri_out, w_bias, single, w_attn, w_out):
    rows_dev, cols_dev, chans = pair.shape
    row_index = lax.axis_index(ROW)
    col_index = lax.axis_index(COL)
    maskf = mask.astype(jnp.float32)
    row_mask = lax.dynamic_slice_in_dim(maskf, row_index * rows_dev, rows_dev)
    col_mask = lax.dynamic_slice_in_dim(maskf, col_index * cols_dev, cols_dev)
    pair_mask = row_mask[:, None] * col_mask[None, :]
    pair_f = pair.astype(jnp.float32)
    normed = layer_norm(pair_f, 2).astype(jnp.bfloat16)
    leading = jnp.einsum(
        "ijc,cd->dij", normed, w_tri_in[:, : 4 * chans], preferred_element_type=jnp.float32
    )
    left = (jax.nn.sigmoid(leading[chans : 2 * chans]) * leading[:chans] * pair_mask).astype(
        jnp.bfloat16
    )
    right = (
        jax.nn.sigmoid(leading[3 * chans :]) * leading[2 * chans : 3 * chans] * pair_mask
    ).astype(jnp.bfloat16)
    gate = jax.nn.sigmoid(
        jnp.einsum(
            "ijc,cd->ijd", normed, w_tri_in[:, 4 * chans :], preferred_element_type=jnp.float32
        )
    )
    xn = layer_norm(single.astype(jnp.float32), 2).astype(jnp.bfloat16)
    projected = jnp.einsum("srd,dhe->shre", xn, w_attn, preferred_element_type=jnp.float32)
    query = projected[..., :HEAD_DIM].astype(jnp.bfloat16)
    keyval = projected[..., HEAD_DIM : 3 * HEAD_DIM].astype(jnp.bfloat16)
    packed = keyval[:, 0].reshape(2, 8, rows_dev, 2, HEAD_DIM).transpose(3, 0, 2, 1, 4)
    agate = jax.nn.sigmoid(projected[..., 3 * HEAD_DIM :])
    tri, keyval_all, w_out_all = triangle(
        left.reshape(16, 8, 16, 128),
        right.reshape(16, 8, 16, 128),
        packed.reshape(4, rows_dev, 8 * HEAD_DIM),
        w_out,
    )
    tri_tile = tri.reshape(chans, 16, 2, cols_dev).transpose(0, 2, 1, 3)
    tri_tile = tri_tile.reshape(chans, rows_dev, cols_dev)
    keyval_all = keyval_all.reshape(32, 2, 2, rows_dev, 8, HEAD_DIM).transpose(1, 2, 4, 0, 3, 5)
    keyval_all = keyval_all.reshape(2, 16, 1, 32 * rows_dev, HEAD_DIM)
    tnorm = layer_norm(tri_tile.astype(jnp.float32), 0).astype(jnp.bfloat16)
    update = jnp.einsum("cij,cd->ijd", tnorm, w_tri_out, preferred_element_type=jnp.float32)
    new_pair = (pair_f + gate * update).astype(jnp.bfloat16)
    pnorm = layer_norm(new_pair.astype(jnp.float32), 2).astype(jnp.bfloat16)
    bias_tile = jnp.einsum("ijc,cl->lij", pnorm, w_bias, preferred_element_type=jnp.float32).astype(
        jnp.bfloat16
    )
    bias_tile = bias_tile.reshape(LAYERS, HEADS, rows_dev, cols_dev)
    biases = lax.all_to_all(bias_tile, COL, split_axis=1, concat_axis=3, tiled=True)
    score = jnp.einsum(
        "shqe,shke->shqk", query, keyval_all[0], preferred_element_type=jnp.float32
    )
    score = score * HEAD_DIM ** (-0.5) + biases[0].astype(jnp.float32)[None]
    score = jnp.where((mask > 0)[None, None, None, :], score, -1000000000.0)
    peak = jnp.max(score, axis=3, keepdims=True)
    expo = jnp.exp(score - peak)
    probs = (expo / jnp.sum(expo, axis=3, keepdims=True)).astype(jnp.bfloat16)
    context = jnp.einsum(
        "shqk,shke->shqe", probs, keyval_all[1], preferred_element_type=jnp.float32
    )
    gated = (agate * context).astype(jnp.bfloat16)
    heads_out = lax.all_to_all(gated[:, 0], COL, split_axis=0, concat_axis=2, tiled=True)
    attended = jnp.einsum(
        "sqd,cde->sqce",
        heads_out,
        w_out_all.reshape(2, HEADS * HEAD_DIM, 384),
        preferred_element_type=jnp.float32,
    )
    attended = attended.astype(jnp.bfloat16).reshape(1, rows_dev, 768)
    return (new_pair, biases, attended)


def solution(mesh):
    fine = Mesh(mesh.devices.reshape(4, 4, 2, 4, 4), ("z_hi", "x", "core", "y", "z_lo"))
    placed = (
        P(ROW, COL, None),
        P(),
        P(),
        P(),
        P(),
        P(None, ROW, None),
        P(None, COL, None),
        P(COL, None),
    )
    return jax.shard_map(
        per_device,
        mesh=fine,
        in_specs=placed,
        out_specs=(P(ROW, COL, None), P(None, COL, ROW, None), P(COL, ROW, None)),
        check_vma=False,
    )
```

time: 503 us -> 246 us (0.49)
  waiting for transfers between devices: 366 us -> 6.67 us
  Pallas kernels: 0 us -> 112 us
  local copies, waits for them, and re-layouts: 16.3 us -> 84.8 us
  blocking collectives: 45.4 us -> 0 us
  starting transfers between devices: 31.1 us -> 13 us
  between operations: 14.2 us -> 1.05 us
  matrix products: 23 us -> 13.8 us
    all_gather x2 -> x0, waiting for transfers between devices: 192 us -> none  [the longest x1 163 us: per_device(): lax.all_gather(left_full, 'col', axis=2, tiled=True)]
    pallas_call x0 -> x1, Pallas kernels: none -> 112 us  [triangle(): pl.pallas_call(triangle_kernel, out_shape=(jax.ShapeDtypeStruct((16, 8, 1...]
    reduce_scatter x1 -> x0, waiting for transfers between devices: 85.4 us -> none  [per_device(): lax.psum_scatter(jnp.einsum('shqe,hed->sqd', gated, out_local, preferred_...]
    all_to_all x3 -> x2, waiting for transfers between devices: 88.6 us -> 6.67 us  [the longest x1 6.67 us: per_device(): lax.all_to_all(gated[:, 0], COL, split_axis=0, concat_axis=2, tiled=True)]
    all_to_all x1 -> x0, blocking collectives: 45.4 us -> none  [per_device(): lax.all_to_all(left, 'row', split_axis=0, concat_axis=1, tiled=True)]
    reshape x0 -> x5, local copies, waits for them, and re-layouts: none -> 25.7 us  [the longest x1 22.3 us: per_device(): keyval_all.reshape(32, 2, 2, rows_dev, 8, HEAD_DIM)]
    another operation x0 -> x5, local copies, waits for them, and re-layouts: none -> 19.8 us
    all_to_all x3 -> x2, starting transfers between devices: 30.6 us -> 13 us  [the longest x1 7.46 us: per_device(): lax.all_to_all(gated[:, 0], COL, split_axis=0, concat_axis=2, tiled=True)]
  transfers between devices with their start and end apart: 6 -> 2, of which waited for: 6 -> 1; matrix products, arithmetic and copies ran while one was open for 5% -> 22% of each run, Pallas kernels for 0% -> 0%
where the time goes in v1:
time: 246 us; the launch traced here: 243 us
  Pallas kernels  112 us (46%)
  local copies, waits for them, and re-layouts  84.8 us (34%)
  matrix products  13.8 us (6%)
  starting transfers between devices  13 us (5%)
  other arithmetic  11.4 us (5%)
  waiting for transfers between devices  6.67 us (3%)
    pallas_call x1, Pallas kernels, triangle(): pl.pallas_call(triangle_kernel, out_shape=(jax.ShapeDtypeStruct((16, 8, 1...  112 us
    reshape x1, local copies, waits for them, and re-layouts, per_device(): keyval_all.reshape(32, 2, 2, rows_dev, 8, HEAD_DIM)  22.3 us
    another operation x3, local copies, waits for them, and re-layouts  19.5 us
    slice x1, local copies, waits for them, and re-layouts, per_device(): keyval_all[0]  11.7 us
    unnamed x42, local copies, waits for them, and re-layouts  10.6 us
    all_to_all x1, starting transfers between devices, per_device(): lax.all_to_all(gated[:, 0], COL, split_axis=0, concat_axis=2, tiled=True)  7.46 us
    convert_element_type x2, local copies, waits for them, and re-layouts, per_device(): tnorm = layer_norm(tri_tile.astype(jnp.float32), 0).astype(jnp.bfloat16)  7.26 us
    all_to_all x1, waiting for transfers between devices, per_device(): lax.all_to_all(gated[:, 0], COL, split_axis=0, concat_axis=2, tiled=True)  6.67 us
  transfers between devices with their start and end apart: 2, of which 1 were waited for; matrix products, arithmetic and copies ran while one was open for 22% of the time, Pallas kernels for 0%

profile of v1, /device:TPU:6, one launch (start us, length us, event | category | flops | bytes accessed | tf_op | source)
XLA Modules:
  0.0 242.5 jit_solution(17180518371823451766)
XLA Ops:
  2.9 1.7 fusion.19
  5.3 2.0 convolution_bitcast_fusion
  7.9 1.6 copy.54
  10.8 1.6 copy.55
  19.7 111.7 %triangle.1 = (bf16[16,8,16,128]{3,2,1,0:T(8,128)(2,1)S(1)}, bf16[16,2,4,32,384]{4,3,2,1,0:T(8,128)(2,1)S(1)}, bf16[2,16,48,384]{3,2,1,0:T(8,128)(2,1)S(1)}) custom-call(bf16[16,8,16,128]{3,2,1,0:T(8,128)(2,1)S(1)} %copy-done.1, bf16[16,8,16,128]{3,2,1,0:T(8,128)(2,1)S(1)} %copy-done.2, bf16[4,32,384]{2,1,0:T(8,128)(2,1)S(1)} %reshape.195.keyval_in, ...), custom_call_target="tpu_custom_call" | custom-call | tf_op jit(solution)/shard_map/triangle/pallas_call | solution.py:176
  133.3 3.3 %reshape.207 = f32[128,16,2,64]{3,2,1,0:T(2,128)} reshape(bf16[16,8,16,128]{3,2,1,0:T(8,128)(2,1)} %copy-done.5) | data formatting | bytes 1572864 | tf_op jit(solution)/shard_map/convert_element_type | solution.py:241
  136.6 2.4 %bitcast_reduce_fusion = f32[2,16,64]{2,0,1:T(2,128)S(1)} fusion(f32[128,16,2,64]{3,2,1,0:T(2,128)} %reshape.207), kind=kLoop, calls=%fused_computation.97 | loop fusion | flops 260096 | bytes 1056768 | tf_op jit(solution)/shard_map/reduce_sum | solution.py:17
  139.1 1.4 multiply_reduce_fusion
  140.5 3.9 %copy.57 = f32[128,2,16,64]{0,3,2,1:T(8,128)} copy(f32[128,2,16,64]{3,1,2,0:T(2,128)} %bitcast.114) | data formatting | bytes 2097152 | tf_op jit(solution)/shard_map/convert_element_type | solution.py:241
  144.5 1.9 fusion.34
  146.7 2.1 convert_reduce_fusion.2
  149.6 1.5 fusion.15
  151.1 2.5 %copy.61 = bf16[64,32,64]{2,1,0:T(8,128)(2,1)} copy(bf16[64,32,64]{0,2,1:T(8,128)(2,1)} %fusion.15) | data formatting | bytes 524288 | tf_op jit(solution)/shard_map/convert_element_type | solution.py:245
  153.7 1.9 copy.79
  155.6 2.1 reshape.215
  157.7 5.6 %all-to-all-start = ((bf16[16,2,4096]{2,1,0:T(2,128)(2,1)}), bf16[16,2,4096]{2,1,0:T(2,128)(2,1)}, u32[]{:S(2)}, u32[]{:S(2)}) async-start(bf16[16,2,4096]{2,1,0:T(2,128)(2,1)} %reshape.215), calls=%async_computation | async-start | bytes 524288 | tf_op jit(solution)/shard_map/all_to_all | solution.py:249
  163.3 22.3 %copy.69 = bf16[16,2,4,32,384]{3,1,0,4,2:T(2,128)(2,1)} copy(bf16[16,2,4,32,384]{4,3,2,1,0:T(8,128)(2,1)S(1)} %get-tuple-element.7) | data formatting | bytes 6291456 | tf_op jit(solution)/shard_map/reshape | solution.py:239
  185.6 11.7 %fusion.67 = (bf16[1,2,8,32,32,48]{4,3,5,2,1,0:T(8,128)(2,1)}, bf16[1,2,8,32,32,48]{4,3,5,2,1,0:T(8,128)(2,1)}) fusion(bf16[2,2,8,32,32,48]{4,3,5,2,1,0:T(8,128)(2,1)} %bitcast.113), kind=kLoop, calls=%fused_computation.100 | loop fusion | bytes 6291456 | tf_op jit(solution)/shard_map/slice | solution.py:251
  197.3 9.6 %reshape.199 = bf16[16,1024,48]{1,2,0:T(8,128)(2,1)} reshape(bf16[1,2,8,32,32,48]{4,3,5,2,1,0:T(8,128)(2,1)} %get-tuple-element.18) | data formatting | bytes 3145728 | tf_op jit(solution)/shard_map/reshape.6
  207.0 9.7 %reshape.200 = bf16[16,1024,48]{1,2,0:T(8,128)(2,1)} reshape(bf16[1,2,8,32,32,48]{4,3,5,2,1,0:T(8,128)(2,1)} %get-tuple-element.19) | data formatting | bytes 3145728 | tf_op jit(solution)/shard_map/reshape.29
  218.4 3.7 %fusion.69 = (f32[16,32]{1,0:T(8,128)S(1)}, f32[16,32,1024]{2,1,0:T(8,128)}) fusion(f32[32,1024]{1,0:T(8,128)S(1)} %reshape.205, pred[1024]{0:T(1024)(128)(4,1)S(1)} %broadcast_compare_fusion, bf16[16,1024,48]{1,2,0:T(8,128)(2,1)} %reshape.199, bf16[16,1,32,192]{3,2,0,1:T(8,128)(2,1)S(1)} %copy-done.14), kind=kOutput, calls=%fused_computation.102 | convolution fusion | flops 52954112 | bytes 3935232 | tf_op jit(solution)/shard_map/sub | solution.py:256
  222.1 2.7 %fusion.18 = bf16[16,32,48]{2,1,0:T(8,128)(2,1)S(1)} fusion(bf16[16,1024,48]{1,2,0:T(8,128)(2,1)} %reshape.200, f32[16,32,1024]{2,1,0:T(8,128)} %get-tuple-element.27, f32[16,32]{1,0:T(8,128)S(1)} %get-tuple-element.26, f32[16,1,32,192]{3,2,0,1:T(8,128)S(1)} %copy-done.18), kind=kOutput, calls=%fused_computation.34 | convolution fusion | flops 51503104 | bytes 3819520 | tf_op jit(solution)/shard_map/shqk,shke->shqe/dot_general | solution.py:258
  225.5 7.5 %all-to-all-start.1 = ((bf16[16,2,768]{2,1,0:T(2,128)(2,1)}), bf16[16,2,768]{2,1,0:T(2,128)(2,1)S(1)}, u32[]{:S(2)}, u32[]{:S(2)}) async-start(bf16[16,2,768]{2,1,0:T(2,128)(2,1)} %reshape.217), calls=%async_computation.1 | async-start | bytes 98304 | tf_op jit(solution)/shard_map/all_to_all | solution.py:262
  234.4 6.7 %all-to-all-done.1 = bf16[16,2,768]{2,1,0:T(2,128)(2,1)S(1)} async-done(((bf16[16,2,768]{2,1,0:T(2,128)(2,1)}), bf16[16,2,768]{2,1,0:T(2,128)(2,1)S(1)}, u32[]{:S(2)}, u32[]{:S(2)}) %all-to-all-start.1) | async-done | bytes 49184 | tf_op jit(solution)/shard_map/all_to_all | solution.py:262
  (80 shorter events, 20.3 us)
Async XLA Ops:
  0.6 13.6 %copy-start = (bf16[768,1,192]{0,2,1:T(8,128)(2,1)S(1)}, bf16[768,1,192]{0,2,1:T(8,128)(2,1)}, u32[]{:S(2)}) copy-start(bf16[768,1,192]{0,2,1:T(8,128)(2,1)} %param.14) | copy-start | bytes 884740
  4.6 0.6 copy-start.11
  9.5 4.2 %copy-start.9 = (bf16[16,32,768]{2,1,0:T(8,128)(2,1)S(1)}, bf16[16,32,768]{2,1,0:T(8,128)(2,1)}, u32[]{:S(2)}) copy-start(bf16[16,32,768]{2,1,0:T(8,128)(2,1)} %param.13) | copy-start | bytes 2359300
  15.5 0.7 copy-start.13
  16.7 1.0 copy-start.1
  17.7 1.0 copy-start.2
  18.8 0.9 copy-start.6
  131.4 1.1 copy-start.3
  132.5 0.8 copy-start.5
  136.6 2.5 %copy-start.7 = (f32[128,16,2,64]{3,2,1,0:T(2,128)S(1)}, f32[128,16,2,64]{3,2,1,0:T(2,128)}, u32[]{:S(2)}) copy-start(f32[128,16,2,64]{3,2,1,0:T(2,128)} %reshape.207) | copy-start | bytes 3145732
  140.5 5.8 %copy-start.15 = (bf16[128,128]{1,0:T(8,128)(2,1)S(1)}, bf16[128,128]{1,0:T(8,128)(2,1)}, u32[]{:S(2)}) copy-start(bf16[128,128]{1,0:T(8,128)(2,1)} %param.11) | copy-start | bytes 98308
  144.4 2.2 copy-start.8
  144.4 2.2 copy-start.12
  146.7 2.9 %copy-start.17 = (bf16[128,64]{0,1:T(8,128)(2,1)S(1)}, bf16[128,64]{0,1:T(8,128)(2,1)}, u32[]{:S(2)}) copy-start(bf16[128,64]{0,1:T(8,128)(2,1)} %param.12) | copy-start | bytes 49156
  148.8 0.8 copy-start.10
  157.7 58.9 %all-to-all-start = ((bf16[16,2,4096]{2,1,0:T(2,128)(2,1)}), bf16[16,2,4096]{2,1,0:T(2,128)(2,1)}, u32[]{:S(2)}, u32[]{:S(2)}) async-start(bf16[16,2,4096]{2,1,0:T(2,128)(2,1)} %reshape.215), calls=%async_computation | async-start | bytes 524288 | tf_op jit(solution)/shard_map/all_to_all | solution.py:249
  207.0 9.7 %copy-start.16 = (s32[1024]{0:T(1024)S(1)}, s32[1024]{0:T(1024)}, u32[]{:S(2)}) copy-start(s32[1024]{0:T(1024)} %param.9) | copy-start | bytes 12292
  216.6 1.8 copy-start.14
  218.4 3.7 %copy-start.18 = (f32[16,1,32,192]{3,2,0,1:T(8,128)S(1)}, f32[16,1,32,192]{3,2,0,1:T(8,128)}, u32[]{:S(2)}) copy-start(f32[16,1,32,192]{3,2,0,1:T(8,128)} %get-tuple-element.23) | copy-start | bytes 1179652
  224.7 16.8 %copy-start.4 = (bf16[2,16,48,384]{3,2,1,0:T(8,128)(2,1)S(1)}, bf16[2,16,48,384]{3,2,1,0:T(8,128)(2,1)}, u32[]{:S(2)}) copy-start(bf16[2,16,48,384]{3,2,1,0:T(8,128)(2,1)} %copy-done.3) | copy-start | bytes 3538948
  225.5 15.5 %all-to-all-start.1 = ((bf16[16,2,768]{2,1,0:T(2,128)(2,1)}), bf16[16,2,768]{2,1,0:T(2,128)(2,1)S(1)}, u32[]{:S(2)}, u32[]{:S(2)}) async-start(bf16[16,2,768]{2,1,0:T(2,128)(2,1)} %reshape.217), calls=%async_computation.1 | async-start | bytes 98304 | tf_op jit(solution)/shard_map/all_to_all | solution.py:262

commit v2 on v0

v2 whole, which is shorter than its diff:
```python
import jax
import jax.numpy as jnp
import numpy as np
from jax import lax
from jax.experimental import pallas as pl
from jax.experimental.pallas import tpu as pltpu
from jax.sharding import Mesh
from jax.sharding import PartitionSpec as P

HEADS = 16
HEAD_DIM = 48
LAYERS = 4
WIDE = 8 * HEAD_DIM
ROW = ("z_hi", "x", "core")
COL = ("y", "z_lo")
BF16 = jnp.bfloat16
F32 = jnp.float32

LEFT_X, RIGHT_X, SUM_X = 0, 4, 8
LEFT_Z, RIGHT_Z, SUM_Z, LEFT_Y = 12, 13, 14, 15
OUT_Z, OUT_Y, OUT_CORE = 16, 17, 18
KV_Z, KV_X, KV_CORE = 19, 20, 21
BIAS_FIRST, BIAS_REST, HEADS_OUT = 22, 23, 24
SLOTS = 25


def selections():
    lane = np.arange(4 * WIDE)
    spread = np.arange(4 * HEAD_DIM)[:, None] == lane // WIDE * HEAD_DIM + lane % HEAD_DIM
    gather = np.arange(WIDE)[:, None] % HEAD_DIM == np.arange(128)[None, :]
    own = np.arange(256)[:, None] // 32 == np.arange(WIDE)[None, :] // HEAD_DIM
    return spread.astype(BF16), gather.astype(BF16), own.astype(np.float32)


def layer_norm(value, axis):
    mean = jnp.mean(value, axis=axis, keepdims=True)
    centred = value - mean
    var = jnp.mean(centred * centred, axis=axis, keepdims=True)
    return centred * lax.rsqrt(var + 1e-05)


def each(count, body):
    lax.fori_loop(0, count, lambda step, carry: (body(step), carry)[1], 0)


def wait_bytes(ref, sem):
    pltpu.make_async_copy(ref, ref, sem).wait()


def contract_last(a, b):
    return lax.dot_general(a, b, (((1,), (1,)), ((), ())), preferred_element_type=F32)


def matmul(a, b):
    return jnp.dot(a, b, preferred_element_type=F32)


def whole_kernel(
    pair, mask, w_tri_in, w_tri_out, w_bias, single, w_attn, w_out, spread_in, gather_in, own_in,
    new_pair, biases, attended,
    left_in, right_in, left_x, right_x, left_z, right_z, sums, sums_x, tri,
    left_all, right_own, keyval, keyval_in, w_out_all,
    normed, gate, rows_f, w_in_t, query, agate, score, bias_f, probs,
    bias_in, bias_all, heads_in, heads_all,
    send, recv, local,
):
    z_hi, z_lo = lax.axis_index("z_hi"), lax.axis_index("z_lo")
    x, core, y = lax.axis_index("x"), lax.axis_index("core"), lax.axis_index("y")
    z, xc, head = z_hi * 4 + z_lo, x * 2 + core, y * 4 + z_lo

    def z_place(peer):
        return {"z_hi": lax.div(peer, 4), "z_lo": lax.rem(peer, 4)}

    def xc_place(peer):
        return {"x": lax.div(peer, 2), "core": lax.rem(peer, 2)}

    def col_place(peer):
        return {"y": lax.div(peer, 4), "z_lo": lax.rem(peer, 4)}

    def after(place, step, size):
        return lax.rem(place + 1 + step, size)

    def near(axis, place, step, size):
        return {axis: after(place, step, size)}

    barrier = pltpu.get_barrier_semaphore()

    def greet(peer):
        pl.semaphore_signal(barrier, inc=1, device_id=peer, device_id_type=pl.DeviceIdType.MESH)

    each(15, lambda step: greet(z_place(after(z, step, 16))))
    each(7, lambda step: greet(xc_place(after(xc, step, 8))))
    each(15, lambda step: greet(col_place(after(head, step, 16))))

    def push(src, dst, slot, peer):
        pltpu.make_async_remote_copy(
            src_ref=src, dst_ref=dst, send_sem=send.at[slot], recv_sem=recv.at[slot],
            device_id=peer, device_id_type=pl.DeviceIdType.MESH,
        ).start()

    def keep(src, dst, slot):
        pltpu.make_async_copy(src, dst, local.at[slot]).start()

    def quarter(step):
        return after(z_hi, step, 4)

    def over_x(src, dst, slot, step):
        part = pl.ds(quarter(step) * 4, 4)

        def body(other):
            peer = after(xc, other, 8)
            push(src.at[part, peer], dst.at[part, xc], slot + step, xc_place(peer))

        each(7, body)
        keep(src.at[part, xc], dst.at[part, xc], slot + step)

    def end_x(dst, slot, step):
        wait_bytes(dst.at[0, pl.ds(0, 4)], local.at[slot + step])
        wait_bytes(dst.at[pl.ds(0, 4), pl.ds(0, 7)], recv.at[slot + step])

    def over_z(src, dst, slot, step):
        def body(low):
            peer = quarter(step) * 4 + low

            @pl.when(peer != z)
            def _():
                push(src.at[peer], dst.at[z], slot, z_place(peer))

            @pl.when(peer == z)
            def _():
                keep(src.at[z], dst.at[z], slot)

        each(4, body)

    def end_z(dst, slot):
        wait_bytes(dst.at[pl.ds(0, 1)], local.at[slot])
        wait_bytes(dst.at[pl.ds(0, 15)], recv.at[slot])

    mask_f = mask[...].astype(F32)
    lane = lax.broadcasted_iota(jnp.int32, (1024, 128), 1)
    token = lax.broadcasted_iota(jnp.int32, (1024, 128), 0)
    low_lane = jnp.where(lane < 64, lane, lane - 64)
    chosen = (token == head * 64 + low_lane).astype(F32).astype(BF16)
    col_mask = matmul(jnp.broadcast_to(mask_f, (16, 1024)).astype(BF16), chosen)
    token = lax.broadcasted_iota(jnp.int32, (16, 1024), 1)
    line = lax.broadcasted_iota(jnp.int32, (16, 1024), 0) * 2 + (z_hi * 8 + xc) * 32
    even = jnp.sum(jnp.where(token == line, mask_f, 0.0), axis=1, keepdims=True)
    odd = jnp.sum(jnp.where(token == line + 1, mask_f, 0.0), axis=1, keepdims=True)
    low = lax.broadcasted_iota(jnp.int32, (16, 128), 1) < 64
    cell_mask = jnp.where(low, even, odd) * col_mask

    w_in_t[...] = w_tri_in[:, 0:512].T

    def factor(block, first):
        rows = slice(block * 256, block * 256 + 256)
        both = contract_last(w_in_t[first : first + 256, :], normed[rows, :])
        value = jax.nn.sigmoid(both[128:]) * both[:128]
        for half in range(2):
            line = block * 2 + half
            part = value[:, half * 128 : half * 128 + 128] * cell_mask[line : line + 1]
            rows_f[pl.ds(line, 128, stride=16), :] = part

    for block in range(8):
        rows = slice(block * 256, block * 256 + 256)
        normed[rows, :] = layer_norm(pair[rows, :].astype(F32), 1).astype(BF16)
        factor(block, 0)
    left_in[...] = rows_f[...].astype(BF16).reshape(16, 8, 16, 128)
    pl.semaphore_wait(barrier, 37)
    for step in range(4):
        over_x(left_in, left_x, LEFT_X, step)
    for block in range(8):
        factor(block, 256)
    right_in[...] = rows_f[...].astype(BF16).reshape(16, 8, 16, 128)
    for step in range(4):
        end_x(left_x, LEFT_X, step)
        over_z(left_x, left_z, LEFT_Z, step)
    for step in range(4):
        over_x(right_in, right_x, RIGHT_X, step)
    half_out = w_out.at[:, pl.ds(pl.multiple_of(core * 384, 128), 384)]
    each(3, lambda step: push(half_out, w_out_all.at[core, head], OUT_Z, near("z_lo", z_lo, step, 4)))
    keep(half_out, w_out_all.at[core, head], OUT_Z)
    for step in range(4):
        end_x(right_x, RIGHT_X, step)
        over_z(right_x, right_z, RIGHT_Z, step)

    w_wide = matmul(w_attn[...], spread_in[...]).astype(BF16)
    for group in range(2):
        rows = slice(group * 256, group * 256 + 256)
        xn = layer_norm(single[rows, :].astype(F32), 1).astype(BF16)
        wide = matmul(xn, w_wide)
        query[rows, :] = (wide[:, 0:WIDE] * own_in[...]).astype(BF16)
        for which in range(2):
            part = wide[:, WIDE * (which + 1) : WIDE * (which + 2)] * own_in[...]
            packed = jnp.sum(part.reshape(8, 32, WIDE), axis=0)
            keyval_in[which * 2 + group] = packed.astype(BF16)
        agate[rows, :] = jax.nn.sigmoid(wide[:, 3 * WIDE :])

    mine = keyval.at[z_hi * 4 + x, core]
    each(3, lambda step: push(keyval_in, mine, KV_Z, near("z_hi", z_hi, step, 4)))
    keep(keyval_in, mine, KV_Z)
    wait_bytes(w_out_all.at[0, pl.ds(0, 1)], local.at[OUT_Z])
    wait_bytes(w_out_all.at[0, pl.ds(0, 3)], recv.at[OUT_Z])
    quad = w_out_all.at[core, pl.ds(y * 4, 4)]
    each(3, lambda step: push(quad, quad, OUT_Y, near("y", y, step, 4)))
    for block in range(8):
        rows = slice(block * 256, block * 256 + 256)
        gate[rows, :] = jax.nn.sigmoid(matmul(normed[rows, :], w_tri_in[:, 512:640]))

    def tiles(blocks, z_part, part):
        pieces = [blocks[z_part * 4 + low, :, :, part * 64 : part * 64 + 64] for low in range(4)]
        return jnp.concatenate(pieces, axis=-1).reshape(128, 256)

    end_z(left_z, LEFT_Z)
    for z_part in range(4):
        for part in range(2):
            first = z_part * 256 + part * 128
            left_all[y, :, first : first + 128] = tiles(left_z, z_part, part).T
    own = left_all.at[y]
    each(3, lambda step: push(own, own, LEFT_Y, near("y", y, step, 4)))
    end_z(right_z, RIGHT_Z)
    for z_part in range(4):
        for part in range(2):
            first = z_part * 256 + part * 128
            right_own[first : first + 128, :] = tiles(right_z, z_part, part)
    wait_bytes(left_all.at[pl.ds(0, 3)], recv.at[LEFT_Y])
    for step in range(4):
        part = quarter(step)
        product = matmul(left_all[part], right_own[...]).astype(BF16).reshape(8, 2, 16, 256)
        for low in range(4):
            cut = slice(low * 64, low * 64 + 64)
            sums[part * 4 + low] = jnp.concatenate(
                [product[:, 0, :, cut], product[:, 1, :, cut]], axis=-1
            )
        over_x(sums, sums_x, SUM_X, step)
    for step in range(4):
        end_x(sums_x, SUM_X, step)
        over_z(sums_x, tri, SUM_Z, step)
    wait_bytes(keyval.at[pl.ds(0, 1), 0], local.at[KV_Z])
    wait_bytes(keyval.at[pl.ds(0, 3), 0], recv.at[KV_Z])

    def pass_on(part):
        block = keyval.at[part * 4 + x, core]
        each(3, lambda step: push(block, block, KV_X, near("x", x, step, 4)))

    each(4, pass_on)
    wait_bytes(w_out_all.at[0, pl.ds(0, 12)], recv.at[OUT_Y])
    push(w_out_all.at[core], w_out_all.at[core], OUT_CORE, {"core": 1 - core})
    wait_bytes(keyval.at[pl.ds(0, 12), 0], recv.at[KV_X])
    push(keyval.at[:, core], keyval.at[:, core], KV_CORE, {"core": 1 - core})

    end_z(tri, SUM_Z)
    rows_f[...] = tri[...].reshape(2048, 128).astype(F32)
    w_bias_t = w_bias[...].T
    for block in range(8):
        lines = (block * 2, block * 2 + 16, block * 2 + 1, block * 2 + 17)
        value = jnp.concatenate(
            [rows_f[pl.ds(block * 2 + half, 128, stride=16), :] for half in range(2)], axis=1
        )
        tnorm = layer_norm(value, 0).T.astype(BF16)
        update = matmul(tnorm, w_tri_out[...])
        updated = []
        for place, line in enumerate(lines):
            cells = slice(line * 64, line * 64 + 64)
            change = gate[cells, :] * update[place * 64 : place * 64 + 64]
            updated.append((pair[cells, :].astype(F32) + change).astype(BF16))
            new_pair[cells, :] = updated[-1]
        pnorm = layer_norm(jnp.concatenate(updated, axis=0).astype(F32), 1).astype(BF16)
        bias = contract_last(w_bias_t, pnorm)
        for half in range(2):
            rows = pl.ds(block * 2 + half, 64, stride=16)
            bias_f[rows, :] = bias[:, half * 128 : half * 128 + 128]
    bias_in[...] = bias_f[...].astype(BF16).reshape(4, 16, 16, 128)

    def send_bias(layers, slot):
        def body(step):
            peer = after(head, step, 16)
            push(bias_in.at[layers, peer], bias_all.at[layers, head], slot, col_place(peer))

        each(15, body)
        keep(bias_in.at[layers, head], bias_all.at[layers, head], slot)

    send_bias(pl.ds(0, 1), BIAS_FIRST)
    send_bias(pl.ds(1, 3), BIAS_REST)
    wait_bytes(keyval.at[:, 0], recv.at[KV_CORE])
    for group in range(2):
        rows = slice(group * 256, group * 256 + 256)
        keys = keyval[:, :, group].reshape(1024, WIDE)
        score[rows, :] = contract_last(query[rows, :], keys)

    def bias_rows(layer):
        return jnp.concatenate(
            [
                jnp.concatenate(
                    [bias_all[layer, src, :, part * 64 : part * 64 + 64] for src in range(16)],
                    axis=-1,
                )
                for part in range(2)
            ],
            axis=0,
        )

    wait_bytes(bias_all.at[0, pl.ds(0, 1)], local.at[BIAS_FIRST])
    wait_bytes(bias_all.at[0, pl.ds(0, 15)], recv.at[BIAS_FIRST])
    first_bias = bias_rows(0)
    biases[0] = first_bias
    first_bias = first_bias.astype(F32)
    present = mask_f > 0.0
    for sample in range(16):
        rows = slice(sample * 32, sample * 32 + 32)
        logits = score[rows, :] * HEAD_DIM ** (-0.5) + first_bias
        logits = jnp.where(present, logits, -1000000000.0)
        expo = jnp.exp(logits - jnp.max(logits, axis=1, keepdims=True))
        probs[rows, :] = (expo * (1.0 / jnp.sum(expo, axis=1, keepdims=True))).astype(BF16)
    for group in range(2):
        rows = slice(group * 256, group * 256 + 256)
        values = keyval[:, :, 2 + group].reshape(1024, WIDE)
        context = matmul(probs[rows, :], values)
        gated = (agate[rows, :] * context * own_in[...]).astype(BF16)
        gathered = matmul(gated, gather_in[...]).astype(BF16)
        heads_in[group * 8 : group * 8 + 8] = gathered.reshape(8, 32, 128)

    def send_heads(step):
        peer = after(head, step, 16)
        push(heads_in.at[peer], heads_all.at[head], HEADS_OUT, col_place(peer))

    each(15, send_heads)
    keep(heads_in.at[head], heads_all.at[head], HEADS_OUT)
    wait_bytes(bias_all.at[pl.ds(0, 3), 0], local.at[BIAS_REST])
    wait_bytes(bias_all.at[pl.ds(0, 3), pl.ds(0, 15)], recv.at[BIAS_REST])
    for layer in range(1, 4):
        biases[layer] = bias_rows(layer)
    wait_bytes(w_out_all.at[0], recv.at[OUT_CORE])
    wait_bytes(heads_all.at[pl.ds(0, 1)], local.at[HEADS_OUT])
    wait_bytes(heads_all.at[pl.ds(0, 15)], recv.at[HEADS_OUT])
    merged = jnp.concatenate([heads_all[src, :, 0:HEAD_DIM] for src in range(16)], axis=-1)
    for half in range(2):
        weights = w_out_all[half].reshape(HEADS * HEAD_DIM, 384)
        attended[:, half * 384 : half * 384 + 384] = matmul(merged, weights).astype(BF16)

    for slot in (LEFT_X, RIGHT_X, SUM_X):
        for step in range(4):
            wait_bytes(left_x.at[pl.ds(0, 4), pl.ds(0, 7)], send.at[slot + step])
    for slot in (LEFT_Z, RIGHT_Z, SUM_Z):
        wait_bytes(left_z.at[pl.ds(0, 15)], send.at[slot])
    wait_bytes(left_all.at[pl.ds(0, 3)], send.at[LEFT_Y])
    wait_bytes(w_out_all.at[0, pl.ds(0, 3)], send.at[OUT_Z])
    wait_bytes(w_out_all.at[0, pl.ds(0, 12)], send.at[OUT_Y])
    wait_bytes(w_out_all.at[0], send.at[OUT_CORE])
    wait_bytes(keyval.at[pl.ds(0, 3), 0], send.at[KV_Z])
    wait_bytes(keyval.at[pl.ds(0, 12), 0], send.at[KV_X])
    wait_bytes(keyval.at[:, 0], send.at[KV_CORE])
    wait_bytes(bias_all.at[0, pl.ds(0, 15)], send.at[BIAS_FIRST])
    wait_bytes(bias_all.at[pl.ds(0, 3), pl.ds(0, 15)], send.at[BIAS_REST])
    wait_bytes(heads_all.at[pl.ds(0, 15)], send.at[HEADS_OUT])


def per_device(pair, mask, w_tri_in, w_tri_out, w_bias, single, w_attn, w_out):
    vmem = pl.BlockSpec(memory_space=pltpu.VMEM)
    blocks = pltpu.VMEM((16, 8, 16, 128), BF16)
    new_pair, biases, attended = pl.pallas_call(
        whole_kernel,
        out_shape=(
            jax.ShapeDtypeStruct((2048, 128), BF16),
            jax.ShapeDtypeStruct((LAYERS, 32, 1024), BF16),
            jax.ShapeDtypeStruct((32, 768), BF16),
        ),
        in_specs=[vmem] * 11,
        out_specs=(vmem, vmem, vmem),
        scratch_shapes=[blocks] * 9
        + [
            pltpu.VMEM((4, 256, 1024), BF16),
            pltpu.VMEM((1024, 256), BF16),
            pltpu.VMEM((16, 2, 4, 32, WIDE), BF16),
            pltpu.VMEM((4, 32, WIDE), BF16),
            pltpu.VMEM((2, HEADS, HEAD_DIM, 384), BF16),
            pltpu.VMEM((2048, 128), BF16),
            pltpu.VMEM((2048, 128), F32),
            pltpu.VMEM((2048, 128), F32),
            pltpu.VMEM((512, 128), BF16),
            pltpu.VMEM((512, WIDE), BF16),
            pltpu.VMEM((512, WIDE), F32),
            pltpu.VMEM((512, 1024), F32),
            pltpu.VMEM((1024, 128), F32),
            pltpu.VMEM((512, 1024), BF16),
            pltpu.VMEM((LAYERS, 16, 16, 128), BF16),
            pltpu.VMEM((LAYERS, 16, 16, 128), BF16),
            pltpu.VMEM((16, 32, 128), BF16),
            pltpu.VMEM((16, 32, 128), BF16),
            pltpu.SemaphoreType.DMA((SLOTS,)),
            pltpu.SemaphoreType.DMA((SLOTS,)),
            pltpu.SemaphoreType.DMA((SLOTS,)),
        ],
        compiler_params=pltpu.CompilerParams(
            collective_id=0, has_side_effects=True, vmem_limit_bytes=48 * 1024 * 1024
        ),
        name="whole",
    )(
        pair.reshape(2048, 128),
        mask.reshape(1, 1024),
        w_tri_in,
        w_tri_out,
        w_bias,
        single.reshape(512, 768),
        w_attn.reshape(768, 4 * HEAD_DIM),
        w_out,
        *(jnp.asarray(matrix) for matrix in selections()),
    )
    return (
        new_pair.reshape(32, 64, 128),
        biases.reshape(LAYERS, 1, 32, 1024),
        attended.reshape(1, 32, 768),
    )


def solution(mesh):
    fine = Mesh(mesh.devices.reshape(4, 4, 2, 4, 4), ("z_hi", "x", "core", "y", "z_lo"))
    placed = (
        P(ROW, COL, None),
        P(),
        P(),
        P(),
        P(),
        P(None, ROW, None),
        P(None, COL, None),
        P(COL, None),
    )
    return jax.shard_map(
        per_device,
        mesh=fine,
        in_specs=placed,
        out_specs=(P(ROW, COL, None), P(None, COL, ROW, None), P(COL, ROW, None)),
        check_vma=False,
    )
```

time: 503 us -> 147 us (0.29)
  waiting for transfers between devices: 366 us -> 0 us
  Pallas kernels: 0 us -> 137 us
  blocking collectives: 45.4 us -> 0 us
  starting transfers between devices: 31.1 us -> 0 us
  matrix products: 23 us -> 0 us
  between operations: 14.2 us -> 0.72 us
  local copies, waits for them, and re-layouts: 16.3 us -> 9.16 us
  other arithmetic: 6.87 us -> 0 us
    all_gather x2 -> x0, waiting for transfers between devices: 192 us -> none  [the longest x1 163 us: per_device(): lax.all_gather(left_full, 'col', axis=2, tiled=True)]
    pallas_call x0 -> x1, Pallas kernels: none -> 137 us  [per_device(): pl.pallas_call(whole_kernel, out_shape=(jax.ShapeDtypeStruct((2048, 128),...]
    all_to_all x3 -> x0, waiting for transfers between devices: 88.6 us -> none  [the longest x1 35.4 us: per_device(): lax.all_to_all(summed.astype(jnp.bfloat16), 'row', split_axis=1, concat_a...]
    reduce_scatter x1 -> x0, waiting for transfers between devices: 85.4 us -> none  [per_device(): lax.psum_scatter(jnp.einsum('shqe,hed->sqd', gated, out_local, preferred_...]
    all_to_all x1 -> x0, blocking collectives: 45.4 us -> none  [per_device(): lax.all_to_all(left, 'row', split_axis=0, concat_axis=1, tiled=True)]
    all_to_all x3 -> x0, starting transfers between devices: 30.6 us -> none  [the longest x1 14.2 us: per_device(): lax.all_to_all(summed.astype(jnp.bfloat16), 'row', split_axis=1, concat_a...]
    dot_general x7 -> x0, matrix products: 17.8 us -> none  [the longest x1 6.04 us: per_device(): jnp.einsum('cki,ckj->cij', lax.all_gather(left_full, 'col', axis=2, tiled...]
    convert_element_type x7 -> x0, local copies, waits for them, and re-layouts: 5.24 us -> none  [the longest x1 1.62 us: per_device(): (jax.nn.sigmoid(leading[chans:2 * chans]) * leading[:chans] * pair_mask)....]
  transfers between devices with their start and end apart: 6 -> 0, of which waited for: 6 -> 0; matrix products, arithmetic and copies ran while one was open for 5% -> 0% of each run, Pallas kernels for 0% -> 0%
where the time goes in v2:
time: 147 us; the launch traced here: 146 us
  Pallas kernels  137 us (93%)
  local copies, waits for them, and re-layouts  9.16 us (6%)
    pallas_call x1, Pallas kernels, per_device(): pl.pallas_call(whole_kernel, out_shape=(jax.ShapeDtypeStruct((2048, 128),...  137 us
    unnamed x23, local copies, waits for them, and re-layouts  9.16 us

profile of v2, /device:TPU:6, one launch (start us, length us, event | category | flops | bytes accessed | tf_op | source)
XLA Modules:
  0.0 146.4 jit_solution(15704863486028862283)
XLA Ops:
  0.6 0.0 copy-start.1
  0.6 0.9 copy.15.w_bias
  1.5 0.0 copy-start.5
  1.5 0.0 copy-start.7
  1.6 0.0 copy-start.8
  1.6 1.2 copy.14
  2.7 0.0 copy-done.1
  2.7 0.0 copy-done.5
  2.8 0.0 copy-done.7
  2.8 0.0 copy-done.8
  2.8 0.0 copy-start
  2.8 1.1 copy-done
  3.9 0.0 copy-start.2
  3.9 1.0 copy-done.2
  5.0 0.0 copy-start.3
  5.0 1.0 copy-done.3
  6.0 0.0 copy-start.4
  6.0 0.9 copy-done.4
  6.9 0.0 copy-start.6
  6.9 0.9 copy-done.6
  7.8 136.5 %whole.1 = (bf16[2048,128]{1,0:T(8,128)(2,1)S(1)}, bf16[4,32,1024]{2,1,0:T(8,128)(2,1)S(1)}, bf16[32,768]{1,0:T(8,128)(2,1)S(1)}) custom-call(bf16[2048,128]{1,0:T(8,128)(2,1)S(1)} %bitcast.12, s32[1,1024]{1,0:T(1,128)S(1)} %bitcast.15, bf16[128,640]{1,0:T(8,128)(2,1)S(1)} %copy-done.4, bf16[128,128]{1,0:T(8,128)(2,1)S(1)} %copy-done.7, ...), custom_call_target="tpu_custom_call" | custom-call | tf_op jit(solution)/shard_map/whole/pallas_call | solution.py:360
  144.3 0.8 copy.20
  145.1 0.7 copy.21
  145.8 0.6 copy.22
Async XLA Ops:
  0.6 2.1 %copy-start.1 = (bf16[192,1536]{1,0:T(8,128)(2,1)S(1)}, bf16[192,1536]{1,0:T(8,128)(2,1)}, u32[]{:S(2)}) copy-start(bf16[192,1536]{1,0:T(8,128)(2,1)} %constant.6.clone.spread_in) | copy-start | bytes 1769476
  1.5 1.2 copy-start.5
  1.5 1.2 copy-start.7
  1.6 1.2 copy-start.8
  2.8 1.1 copy-start
  3.9 1.0 copy-start.2
  5.0 1.0 copy-start.3
  6.0 0.9 copy-start.4
  6.9 0.9 copy-start.6

commit v3 on v2

--- a/solution.py
+++ b/solution.py
@@ -1,6 +1,5 @@
 import jax
 import jax.numpy as jnp
-import numpy as np
 from jax import lax
 from jax.experimental import pallas as pl
 from jax.experimental.pallas import tpu as pltpu
@@ -17,19 +16,15 @@
 F32 = jnp.float32
 
 LEFT_X, RIGHT_X, SUM_X = 0, 4, 8
-LEFT_Z, RIGHT_Z, SUM_Z, LEFT_Y = 12, 13, 14, 15
-OUT_Z, OUT_Y, OUT_CORE = 16, 17, 18
-KV_Z, KV_X, KV_CORE = 19, 20, 21
-BIAS_FIRST, BIAS_REST, HEADS_OUT = 22, 23, 24
-SLOTS = 25
-
-
-def selections():
-    lane = np.arange(4 * WIDE)
-    spread = np.arange(4 * HEAD_DIM)[:, None] == lane // WIDE * HEAD_DIM + lane % HEAD_DIM
-    gather = np.arange(WIDE)[:, None] % HEAD_DIM == np.arange(128)[None, :]
-    own = np.arange(256)[:, None] // 32 == np.arange(WIDE)[None, :] // HEAD_DIM
-    return spread.astype(BF16), gather.astype(BF16), own.astype(np.float32)
+LEFT_Z, RIGHT_Z, SUM_Z = 12, 13, 14
+OUT_Z, OUT_Y, OUT_CORE, KV_CORE = 15, 16, 17, 18
+BIAS_FIRST, BIAS_REST, HEADS_OUT = 19, 20, 21
+LEFT_NEAR, LEFT_FAR, KV_Z_NEAR, KV_Z_FAR, KV_X_NEAR, KV_X_FAR = 22, 24, 26, 28, 30, 32
+SLOTS = 34
+
+
+def block_of(index):
+    return sum((index >= HEAD_DIM * edge).astype(jnp.int32) for edge in range(1, 32))
 
 
 def layer_norm(value, axis):
@@ -56,13 +51,15 @@
 
 
 def whole_kernel(
-    pair, mask, w_tri_in, w_tri_out, w_bias, single, w_attn, w_out, spread_in, gather_in, own_in,
+    pair_h, mask_h, w_tri_in_h, w_tri_out_h, w_bias_h, single_h, w_attn_h, w_out_h,
     new_pair, biases, attended,
+    pair, mask, w_tri_in, w_tri_out, w_bias, single, w_attn, w_out,
     left_in, right_in, left_x, right_x, left_z, right_z, sums, sums_x, tri,
+    gather_in, own_in,
     left_all, right_own, keyval, keyval_in, w_out_all,
     normed, gate, rows_f, w_in_t, query, agate, score, bias_f, probs,
     bias_in, bias_all, heads_in, heads_all,
-    send, recv, local,
+    send, recv, local, load,
 ):
     z_hi, z_lo = lax.axis_index("z_hi"), lax.axis_index("z_lo")
     x, core, y = lax.axis_index("x"), lax.axis_index("core"), lax.axis_index("y")
@@ -83,6 +80,17 @@
     def near(axis, place, step, size):
         return {axis: after(place, step, size)}
 
+    loads = [
+        pltpu.make_async_copy(src, dst, load.at[slot])
+        for slot, (src, dst) in enumerate(
+            (
+                (pair_h, pair), (w_tri_in_h, w_tri_in), (mask_h, mask), (w_out_h, w_out),
+                (w_attn_h, w_attn), (single_h, single), (w_tri_out_h, w_tri_out), (w_bias_h, w_bias),
+            )
+        )
+    ]
+    for copy in loads:
+        copy.start()
     barrier = pltpu.get_barrier_semaphore()
 
     def greet(peer):
@@ -136,6 +144,8 @@
         wait_bytes(dst.at[pl.ds(0, 1)], local.at[slot])
         wait_bytes(dst.at[pl.ds(0, 15)], recv.at[slot])
 
+    for copy in loads[:3]:
+        copy.wait()
     mask_f = mask[...].astype(F32)
     lane = lax.broadcasted_iota(jnp.int32, (1024, 128), 1)
     token = lax.broadcasted_iota(jnp.int32, (1024, 128), 0)
@@ -176,6 +186,7 @@
         over_z(left_x, left_z, LEFT_Z, step)
     for step in range(4):
         over_x(right_in, right_x, RIGHT_X, step)
+    loads[3].wait()
     half_out = w_out.at[:, pl.ds(pl.multiple_of(core * 384, 128), 384)]
     each(3, lambda step: push(half_out, w_out_all.at[core, head], OUT_Z, near("z_lo", z_lo, step, 4)))
     keep(half_out, w_out_all.at[core, head], OUT_Z)
@@ -183,7 +194,21 @@
         end_x(right_x, RIGHT_X, step)
         over_z(right_x, right_z, RIGHT_Z, step)
 
-    w_wide = matmul(w_attn[...], spread_in[...]).astype(BF16)
+    for copy in loads[4:]:
+        copy.wait()
+    lane = lax.broadcasted_iota(jnp.int32, (1, 4 * WIDE), 1)
+    block = block_of(lane)
+    source = lane - HEAD_DIM * block + HEAD_DIM * sum((block >= 8 * n).astype(jnp.int32) for n in (1, 2, 3))
+    place = lax.broadcasted_iota(jnp.int32, (4 * HEAD_DIM, 4 * WIDE), 0)
+    spread = (place == source).astype(F32).astype(BF16)
+    place = lax.broadcasted_iota(jnp.int32, (256, WIDE), 0)
+    own_block = ((place >= 32 * block[:, :WIDE]) & (place < 32 * block[:, :WIDE] + 32)).astype(F32)
+    lane = lax.broadcasted_iota(jnp.int32, (WIDE, 128), 1)
+    place = lax.broadcasted_iota(jnp.int32, (WIDE, 128), 0)
+    gather = (place - HEAD_DIM * block_of(place) == lane).astype(F32).astype(BF16)
+    own_in[...] = own_block
+    gather_in[...] = gather
+    w_wide = matmul(w_attn[...].T, spread).astype(BF16)
     for group in range(2):
         rows = slice(group * 256, group * 256 + 256)
         xn = layer_norm(single[rows, :].astype(F32), 1).astype(BF16)
@@ -195,9 +220,6 @@
             keyval_in[which * 2 + group] = packed.astype(BF16)
         agate[rows, :] = jax.nn.sigmoid(wide[:, 3 * WIDE :])
 
-    mine = keyval.at[z_hi * 4 + x, core]
-    each(3, lambda step: push(keyval_in, mine, KV_Z, near("z_hi", z_hi, step, 4)))
-    keep(keyval_in, mine, KV_Z)
     wait_bytes(w_out_all.at[0, pl.ds(0, 1)], local.at[OUT_Z])
     wait_bytes(w_out_all.at[0, pl.ds(0, 3)], recv.at[OUT_Z])
     quad = w_out_all.at[core, pl.ds(y * 4, 4)]
@@ -216,13 +238,27 @@
             first = z_part * 256 + part * 128
             left_all[y, :, first : first + 128] = tiles(left_z, z_part, part).T
     own = left_all.at[y]
-    each(3, lambda step: push(own, own, LEFT_Y, near("y", y, step, 4)))
+    up, down = after(y, 0, 4), after(y, 2, 4)
+    push(own, own, LEFT_NEAR, {"y": up})
+    push(own, own, LEFT_NEAR + 1, {"y": down})
+    wait_bytes(own, recv.at[LEFT_NEAR])
+    passed = left_all.at[down, pl.ds(0, 128)]
+    push(passed, passed, LEFT_FAR, {"y": up})
+    wait_bytes(own, recv.at[LEFT_NEAR + 1])
+    passed = left_all.at[up, pl.ds(128, 128)]
+    push(passed, passed, LEFT_FAR + 1, {"y": down})
     end_z(right_z, RIGHT_Z)
+    mine = keyval.at[z_hi * 4 + x, core]
+    z_up, z_down, x_up, x_down = after(z_hi, 0, 4), after(z_hi, 2, 4), after(x, 0, 4), after(x, 2, 4)
+    push(keyval_in, mine, KV_Z_NEAR, {"z_hi": z_up})
+    push(keyval_in, mine, KV_Z_NEAR + 1, {"z_hi": z_down})
+    keep(keyval_in, mine, KV_Z_NEAR)
     for z_part in range(4):
         for part in range(2):
             first = z_part * 256 + part * 128
             right_own[first : first + 128, :] = tiles(right_z, z_part, part)
-    wait_bytes(left_all.at[pl.ds(0, 3)], recv.at[LEFT_Y])
+    wait_bytes(left_all.at[0, pl.ds(0, 128)], recv.at[LEFT_FAR])
+    wait_bytes(left_all.at[0, pl.ds(0, 128)], recv.at[LEFT_FAR + 1])
     for step in range(4):
         part = quarter(step)
         product = matmul(left_all[part], right_own[...]).astype(BF16).reshape(8, 2, 16, 256)
@@ -235,22 +271,42 @@
     for step in range(4):
         end_x(sums_x, SUM_X, step)
         over_z(sums_x, tri, SUM_Z, step)
-    wait_bytes(keyval.at[pl.ds(0, 1), 0], local.at[KV_Z])
-    wait_bytes(keyval.at[pl.ds(0, 3), 0], recv.at[KV_Z])
-
-    def pass_on(part):
+    wait_bytes(keyval_in, local.at[KV_Z_NEAR])
+    wait_bytes(keyval_in, recv.at[KV_Z_NEAR])
+    passed = keyval.at[z_down * 4 + x, core, pl.ds(0, 2)]
+    push(passed, passed, KV_Z_FAR, {"z_hi": z_up})
+    wait_bytes(keyval_in, recv.at[KV_Z_NEAR + 1])
+    passed = keyval.at[z_up * 4 + x, core, pl.ds(2, 2)]
+    push(passed, passed, KV_Z_FAR + 1, {"z_hi": z_down})
+
+    def over_x_ring(part):
         block = keyval.at[part * 4 + x, core]
-        each(3, lambda step: push(block, block, KV_X, near("x", x, step, 4)))
-
-    each(4, pass_on)
+        push(block, block, KV_X_NEAR, {"x": x_up})
+        push(block, block, KV_X_NEAR + 1, {"x": x_down})
+
+    each(3, lambda step: over_x_ring(lax.rem(z_hi + 3 + step, 4)))
     wait_bytes(w_out_all.at[0, pl.ds(0, 12)], recv.at[OUT_Y])
     push(w_out_all.at[core], w_out_all.at[core], OUT_CORE, {"core": 1 - core})
-    wait_bytes(keyval.at[pl.ds(0, 12), 0], recv.at[KV_X])
+    wait_bytes(keyval_in.at[pl.ds(0, 2)], recv.at[KV_Z_FAR])
+    wait_bytes(keyval_in.at[pl.ds(0, 2)], recv.at[KV_Z_FAR + 1])
+    over_x_ring(lax.rem(z_hi + 2, 4))
+
+    def pass_x(first, src, slot, place):
+        def body(part):
+            passed = keyval.at[part * 4 + src, core, pl.ds(first, 2)]
+            push(passed, passed, slot, place)
+
+        wait_bytes(keyval.at[pl.ds(0, 4), 0], recv.at[slot - 2])
+        each(4, body)
+
+    pass_x(0, x_down, KV_X_FAR, {"x": x_up})
+    pass_x(2, x_up, KV_X_FAR + 1, {"x": x_down})
+    wait_bytes(keyval.at[pl.ds(0, 2), 0], recv.at[KV_X_FAR])
+    wait_bytes(keyval.at[pl.ds(0, 2), 0], recv.at[KV_X_FAR + 1])
     push(keyval.at[:, core], keyval.at[:, core], KV_CORE, {"core": 1 - core})
 
     end_z(tri, SUM_Z)
     rows_f[...] = tri[...].reshape(2048, 128).astype(F32)
-    w_bias_t = w_bias[...].T
     for block in range(8):
         lines = (block * 2, block * 2 + 16, block * 2 + 1, block * 2 + 17)
         value = jnp.concatenate(
@@ -265,7 +321,7 @@
             updated.append((pair[cells, :].astype(F32) + change).astype(BF16))
             new_pair[cells, :] = updated[-1]
         pnorm = layer_norm(jnp.concatenate(updated, axis=0).astype(F32), 1).astype(BF16)
-        bias = contract_last(w_bias_t, pnorm)
+        bias = contract_last(w_bias[...], pnorm)
         for half in range(2):
             rows = pl.ds(block * 2 + half, 64, stride=16)
             bias_f[rows, :] = bias[:, half * 128 : half * 128 + 128]
@@ -342,12 +398,16 @@
             wait_bytes(left_x.at[pl.ds(0, 4), pl.ds(0, 7)], send.at[slot + step])
     for slot in (LEFT_Z, RIGHT_Z, SUM_Z):
         wait_bytes(left_z.at[pl.ds(0, 15)], send.at[slot])
-    wait_bytes(left_all.at[pl.ds(0, 3)], send.at[LEFT_Y])
+    for way in range(2):
+        wait_bytes(left_all.at[0], send.at[LEFT_NEAR + way])
+        wait_bytes(left_all.at[0, pl.ds(0, 128)], send.at[LEFT_FAR + way])
+        wait_bytes(keyval_in, send.at[KV_Z_NEAR + way])
+        wait_bytes(keyval_in.at[pl.ds(0, 2)], send.at[KV_Z_FAR + way])
+        wait_bytes(keyval.at[pl.ds(0, 4), 0], send.at[KV_X_NEAR + way])
+        wait_bytes(keyval.at[pl.ds(0, 2), 0], send.at[KV_X_FAR + way])
     wait_bytes(w_out_all.at[0, pl.ds(0, 3)], send.at[OUT_Z])
     wait_bytes(w_out_all.at[0, pl.ds(0, 12)], send.at[OUT_Y])
     wait_bytes(w_out_all.at[0], send.at[OUT_CORE])
-    wait_bytes(keyval.at[pl.ds(0, 3), 0], send.at[KV_Z])
-    wait_bytes(keyval.at[pl.ds(0, 12), 0], send.at[KV_X])
     wait_bytes(keyval.at[:, 0], send.at[KV_CORE])
     wait_bytes(bias_all.at[0, pl.ds(0, 15)], send.at[BIAS_FIRST])
     wait_bytes(bias_all.at[pl.ds(0, 3), pl.ds(0, 15)], send.at[BIAS_REST])
@@ -364,10 +424,22 @@
             jax.ShapeDtypeStruct((LAYERS, 32, 1024), BF16),
             jax.ShapeDtypeStruct((32, 768), BF16),
         ),
-        in_specs=[vmem] * 11,
+        in_specs=[pl.BlockSpec(memory_space=pltpu.HBM)] * 8,
         out_specs=(vmem, vmem, vmem),
-        scratch_shapes=[blocks] * 9
+        scratch_shapes=[
+            pltpu.VMEM((2048, 128), BF16),
+            pltpu.VMEM((1, 1024), jnp.int32),
+            pltpu.VMEM((128, 640), BF16),
+            pltpu.VMEM((128, 128), BF16),
+            pltpu.VMEM((64, 128), BF16),
+            pltpu.VMEM((512, 768), BF16),
+            pltpu.VMEM((4 * HEAD_DIM, 768), BF16),
+            pltpu.VMEM((HEAD_DIM, 768), BF16),
+        ]
+        + [blocks] * 9
         + [
+            pltpu.VMEM((WIDE, 128), BF16),
+            pltpu.VMEM((256, WIDE), F32),
             pltpu.VMEM((4, 256, 1024), BF16),
             pltpu.VMEM((1024, 256), BF16),
             pltpu.VMEM((16, 2, 4, 32, WIDE), BF16),
@@ -389,9 +461,10 @@
             pltpu.SemaphoreType.DMA((SLOTS,)),
             pltpu.SemaphoreType.DMA((SLOTS,)),
             pltpu.SemaphoreType.DMA((SLOTS,)),
+            pltpu.SemaphoreType.DMA((8,)),
         ],
         compiler_params=pltpu.CompilerParams(
-            collective_id=0, has_side_effects=True, vmem_limit_bytes=48 * 1024 * 1024
+            collective_id=0, has_side_effects=True, vmem_limit_bytes=60 * 1024 * 1024
         ),
         name="whole",
     )(
@@ -399,11 +472,10 @@
         mask.reshape(1, 1024),
         w_tri_in,
         w_tri_out,
-        w_bias,
+        w_bias.T,
         single.reshape(512, 768),
-        w_attn.reshape(768, 4 * HEAD_DIM),
+        w_attn.transpose(1, 2, 0).reshape(4 * HEAD_DIM, 768),
         w_out,
-        *(jnp.asarray(matrix) for matrix in selections()),
     )
     return (
         new_pair.reshape(32, 64, 128),

time: 147 us -> 147 us (level)
  Pallas kernels: 137 us -> 143 us
  local copies, waits for them, and re-layouts: 9.16 us -> 3.33 us
    pallas_call x1, Pallas kernels: 137 us -> 143 us  [per_device(): pl.pallas_call(whole_kernel, out_shape=(jax.ShapeDtypeStruct((2048, 128),...]
    unnamed x23 -> x7, local copies, waits for them, and re-layouts: 9.16 us -> 3.33 us
where the time goes in v3:
time: 147 us
  Pallas kernels  143 us (97%)
  local copies, waits for them, and re-layouts  3.33 us (2%)
    pallas_call x1, Pallas kernels, per_device(): pl.pallas_call(whole_kernel, out_shape=(jax.ShapeDtypeStruct((2048, 128),...  143 us
    unnamed x7, local copies, waits for them, and re-layouts  3.33 us

profile of v3, /device:TPU:6, one launch (start us, length us, event | category | flops | bytes accessed | tf_op | source)
XLA Modules:
  0.0 147.1 jit_solution(5787047235092085618)
XLA Ops:
  0.6 143.1 %whole.1 = (bf16[2048,128]{1,0:T(8,128)(2,1)}, bf16[4,32,1024]{2,1,0:T(8,128)(2,1)}, bf16[32,768]{1,0:T(8,128)(2,1)}) custom-call(bf16[2048,128]{1,0:T(8,128)(2,1)} %bitcast.14, s32[1,1024]{1,0:T(1,128)} %bitcast.19, bf16[128,640]{1,0:T(8,128)(2,1)} %w_tri_in_h.1, bf16[128,128]{1,0:T(8,128)(2,1)} %w_tri_out_h.1, bf16[64,128]{1,0:T(8,128)(2,1)} %bitcast.18, ...), custom_call_target="tpu_custom_call" | custom-call | tf_op jit(solution)/shard_map/whole/pallas_call | solution.py:420
  143.8 0.0 copy-start
  143.8 1.9 %copy.15 = bf16[32,64,128]{2,1,0:T(8,128)(2,1)} copy(bf16[32,64,128]{2,1,0:T(8,128)(2,1)} %bitcast.13) | data formatting | bytes 1048576
  145.7 0.0 copy-done
  145.7 0.0 copy-start.1
  145.7 0.7 copy.16
  146.4 0.1 copy-done.1
  146.5 0.6 copy.17
Async XLA Ops:
  143.8 1.9 %copy-start = (bf16[4,32,1024]{2,1,0:T(8,128)(2,1)S(1)}, bf16[4,32,1024]{2,1,0:T(8,128)(2,1)}, u32[]{:S(2)}) copy-start(bf16[4,32,1024]{2,1,0:T(8,128)(2,1)} %get-tuple-element.7) | copy-start | bytes 786436
  145.7 0.8 copy-start.1

commit v4 on v3

--- a/solution.py
+++ b/solution.py
@@ -16,11 +16,12 @@
 F32 = jnp.float32
 
 LEFT_X, RIGHT_X, SUM_X = 0, 4, 8
-LEFT_Z, RIGHT_Z, SUM_Z = 12, 13, 14
+RIGHT_Z, SUM_Z = 13, 14
 OUT_Z, OUT_Y, OUT_CORE, KV_CORE = 15, 16, 17, 18
 BIAS_FIRST, BIAS_REST, HEADS_OUT = 19, 20, 21
-LEFT_NEAR, LEFT_FAR, KV_Z_NEAR, KV_Z_FAR, KV_X_NEAR, KV_X_FAR = 22, 24, 26, 28, 30, 32
-SLOTS = 34
+LEFT_FAR, KV_Z_NEAR, KV_Z_FAR, KV_X_NEAR, KV_X_FAR = 22, 24, 26, 28, 30
+LEFT_UP, LEFT_DOWN, LEFT_QUARTER = 32, 36, 40
+SLOTS = 44
 
 
 def block_of(index):
@@ -183,16 +184,13 @@
     right_in[...] = rows_f[...].astype(BF16).reshape(16, 8, 16, 128)
     for step in range(4):
         end_x(left_x, LEFT_X, step)
-        over_z(left_x, left_z, LEFT_Z, step)
+        over_z(left_x, left_z, LEFT_QUARTER + step, step)
     for step in range(4):
         over_x(right_in, right_x, RIGHT_X, step)
     loads[3].wait()
     half_out = w_out.at[:, pl.ds(pl.multiple_of(core * 384, 128), 384)]
     each(3, lambda step: push(half_out, w_out_all.at[core, head], OUT_Z, near("z_lo", z_lo, step, 4)))
     keep(half_out, w_out_all.at[core, head], OUT_Z)
-    for step in range(4):
-        end_x(right_x, RIGHT_X, step)
-        over_z(right_x, right_z, RIGHT_Z, step)
 
     for copy in loads[4:]:
         copy.wait()
@@ -220,6 +218,13 @@
             keyval_in[which * 2 + group] = packed.astype(BF16)
         agate[rows, :] = jax.nn.sigmoid(wide[:, 3 * WIDE :])
 
+    def sent_z(slot, step):
+        wait_bytes(left_z.at[pl.ds(0, 3 if step == 3 else 4)], send.at[slot + step])
+
+    for step in range(4):
+        end_x(right_x, RIGHT_X, step)
+        sent_z(LEFT_QUARTER, step)
+        over_z(right_x, right_z, RIGHT_Z, step)
     wait_bytes(w_out_all.at[0, pl.ds(0, 1)], local.at[OUT_Z])
     wait_bytes(w_out_all.at[0, pl.ds(0, 3)], recv.at[OUT_Z])
     quad = w_out_all.at[core, pl.ds(y * 4, 4)]
@@ -232,21 +237,25 @@
         pieces = [blocks[z_part * 4 + low, :, :, part * 64 : part * 64 + 64] for low in range(4)]
         return jnp.concatenate(pieces, axis=-1).reshape(128, 256)
 
-    end_z(left_z, LEFT_Z)
-    for z_part in range(4):
+    up, down = after(y, 0, 4), after(y, 2, 4)
+    for step in range(4):
+        if step == 3:
+            wait_bytes(left_z.at[pl.ds(0, 1)], local.at[LEFT_QUARTER + step])
+        wait_bytes(left_z.at[pl.ds(0, 3 if step == 3 else 4)], recv.at[LEFT_QUARTER + step])
+        source = lax.rem(z_hi + 3 - step, 4)
         for part in range(2):
-            first = z_part * 256 + part * 128
-            left_all[y, :, first : first + 128] = tiles(left_z, z_part, part).T
-    own = left_all.at[y]
-    up, down = after(y, 0, 4), after(y, 2, 4)
-    push(own, own, LEFT_NEAR, {"y": up})
-    push(own, own, LEFT_NEAR + 1, {"y": down})
-    wait_bytes(own, recv.at[LEFT_NEAR])
-    passed = left_all.at[down, pl.ds(0, 128)]
-    push(passed, passed, LEFT_FAR, {"y": up})
-    wait_bytes(own, recv.at[LEFT_NEAR + 1])
-    passed = left_all.at[up, pl.ds(128, 128)]
-    push(passed, passed, LEFT_FAR + 1, {"y": down})
+            left_all[y, source, :, part * 128 : part * 128 + 128] = tiles(left_z, source, part).T
+        own = left_all.at[y, source]
+        push(own, own, LEFT_UP + step, {"y": up})
+        push(own, own, LEFT_DOWN + step, {"y": down})
+    for step in range(4):
+        source = lax.rem(z_hi + 3 - step, 4)
+        wait_bytes(left_all.at[y, 0], recv.at[LEFT_UP + step])
+        passed = left_all.at[down, source, pl.ds(0, 128)]
+        push(passed, passed, LEFT_FAR, {"y": up})
+        wait_bytes(left_all.at[y, 0], recv.at[LEFT_DOWN + step])
+        passed = left_all.at[up, source, pl.ds(128, 128)]
+        push(passed, passed, LEFT_FAR + 1, {"y": down})
     end_z(right_z, RIGHT_Z)
     mine = keyval.at[z_hi * 4 + x, core]
     z_up, z_down, x_up, x_down = after(z_hi, 0, 4), after(z_hi, 2, 4), after(x, 0, 4), after(x, 2, 4)
@@ -257,11 +266,14 @@
         for part in range(2):
             first = z_part * 256 + part * 128
             right_own[first : first + 128, :] = tiles(right_z, z_part, part)
-    wait_bytes(left_all.at[0, pl.ds(0, 128)], recv.at[LEFT_FAR])
-    wait_bytes(left_all.at[0, pl.ds(0, 128)], recv.at[LEFT_FAR + 1])
+    for way in range(2):
+        wait_bytes(left_all.at[0, pl.ds(0, 2)], recv.at[LEFT_FAR + way])
     for step in range(4):
         part = quarter(step)
-        product = matmul(left_all[part], right_own[...]).astype(BF16).reshape(8, 2, 16, 256)
+        product = sum(
+            matmul(left_all[part, quad], right_own[quad * 256 : quad * 256 + 256]) for quad in range(4)
+        )
+        product = product.astype(BF16).reshape(8, 2, 16, 256)
         for low in range(4):
             cut = slice(low * 64, low * 64 + 64)
             sums[part * 4 + low] = jnp.concatenate(
@@ -396,11 +408,12 @@
     for slot in (LEFT_X, RIGHT_X, SUM_X):
         for step in range(4):
             wait_bytes(left_x.at[pl.ds(0, 4), pl.ds(0, 7)], send.at[slot + step])
-    for slot in (LEFT_Z, RIGHT_Z, SUM_Z):
+    for slot in (RIGHT_Z, SUM_Z):
         wait_bytes(left_z.at[pl.ds(0, 15)], send.at[slot])
     for way in range(2):
-        wait_bytes(left_all.at[0], send.at[LEFT_NEAR + way])
-        wait_bytes(left_all.at[0, pl.ds(0, 128)], send.at[LEFT_FAR + way])
+        for step in range(4):
+            wait_bytes(left_all.at[0, 0], send.at[(LEFT_UP, LEFT_DOWN)[way] + step])
+        wait_bytes(left_all.at[0, pl.ds(0, 2)], send.at[LEFT_FAR + way])
         wait_bytes(keyval_in, send.at[KV_Z_NEAR + way])
         wait_bytes(keyval_in.at[pl.ds(0, 2)], send.at[KV_Z_FAR + way])
         wait_bytes(keyval.at[pl.ds(0, 4), 0], send.at[KV_X_NEAR + way])
@@ -440,7 +453,7 @@
         + [
             pltpu.VMEM((WIDE, 128), BF16),
             pltpu.VMEM((256, WIDE), F32),
-            pltpu.VMEM((4, 256, 1024), BF16),
+            pltpu.VMEM((4, 4, 256, 256), BF16),
             pltpu.VMEM((1024, 256), BF16),
             pltpu.VMEM((16, 2, 4, 32, WIDE), BF16),
             pltpu.VMEM((4, 32, WIDE), BF16),

time: 147 us -> 147 us (level)
  no operation moved by 1% of the time
where the time goes in v4:
time: 147 us; the launch traced here: 146 us
  Pallas kernels  142 us (97%)
  local copies, waits for them, and re-layouts  3.33 us (2%)
    pallas_call x1, Pallas kernels, per_device(): pl.pallas_call(whole_kernel, out_shape=(jax.ShapeDtypeStruct((2048, 128),...  142 us
    unnamed x7, local copies, waits for them, and re-layouts  3.33 us

profile of v4, /device:TPU:6, one launch (start us, length us, event | category | flops | bytes accessed | tf_op | source)
XLA Modules:
  0.0 146.2 jit_solution(11604153066507905713)
XLA Ops:
  0.6 142.3 %whole.1 = (bf16[2048,128]{1,0:T(8,128)(2,1)}, bf16[4,32,1024]{2,1,0:T(8,128)(2,1)}, bf16[32,768]{1,0:T(8,128)(2,1)}) custom-call(bf16[2048,128]{1,0:T(8,128)(2,1)} %bitcast.14, s32[1,1024]{1,0:T(1,128)} %bitcast.19, bf16[128,640]{1,0:T(8,128)(2,1)} %w_tri_in_h.1, bf16[128,128]{1,0:T(8,128)(2,1)} %w_tri_out_h.1, bf16[64,128]{1,0:T(8,128)(2,1)} %bitcast.18, ...), custom_call_target="tpu_custom_call" | custom-call | tf_op jit(solution)/shard_map/whole/pallas_call | solution.py:433
  142.9 0.0 copy-start
  142.9 1.9 %copy.15 = bf16[32,64,128]{2,1,0:T(8,128)(2,1)} copy(bf16[32,64,128]{2,1,0:T(8,128)(2,1)} %bitcast.13) | data formatting | bytes 1048576
  144.8 0.0 copy-done
  144.8 0.0 copy-start.1
  144.8 0.7 copy.16
  145.5 0.1 copy-done.1
  145.6 0.6 copy.17
Async XLA Ops:
  142.9 1.9 %copy-start = (bf16[4,32,1024]{2,1,0:T(8,128)(2,1)S(1)}, bf16[4,32,1024]{2,1,0:T(8,128)(2,1)}, u32[]{:S(2)}) copy-start(bf16[4,32,1024]{2,1,0:T(8,128)(2,1)} %get-tuple-element.7) | copy-start | bytes 786436
  144.8 0.8 copy-start.1

commit v5 on v4

--- a/solution.py
+++ b/solution.py
@@ -113,8 +113,8 @@
     def quarter(step):
         return after(z_hi, step, 4)
 
-    def over_x(src, dst, slot, step):
-        part = pl.ds(quarter(step) * 4, 4)
+    def over_x(src, dst, slot, step, first):
+        part = pl.ds(first * 4, 4)
 
         def body(other):
             peer = after(xc, other, 8)
@@ -178,15 +178,12 @@
     left_in[...] = rows_f[...].astype(BF16).reshape(16, 8, 16, 128)
     pl.semaphore_wait(barrier, 37)
     for step in range(4):
-        over_x(left_in, left_x, LEFT_X, step)
+        over_z(left_in, left_z, LEFT_QUARTER + step, step)
     for block in range(8):
         factor(block, 256)
     right_in[...] = rows_f[...].astype(BF16).reshape(16, 8, 16, 128)
     for step in range(4):
-        end_x(left_x, LEFT_X, step)
-        over_z(left_x, left_z, LEFT_QUARTER + step, step)
-    for step in range(4):
-        over_x(right_in, right_x, RIGHT_X, step)
+        over_x(right_in, right_x, RIGHT_X, step, quarter(step))
     loads[3].wait()
     half_out = w_out.at[:, pl.ds(pl.multiple_of(core * 384, 128), 384)]
     each(3, lambda step: push(half_out, w_out_all.at[core, head], OUT_Z, near("z_lo", z_lo, step, 4)))
@@ -225,6 +222,11 @@
         end_x(right_x, RIGHT_X, step)
         sent_z(LEFT_QUARTER, step)
         over_z(right_x, right_z, RIGHT_Z, step)
+    mine = keyval.at[z_hi * 4 + x, core]
+    z_up, z_down, x_up, x_down = after(z_hi, 0, 4), after(z_hi, 2, 4), after(x, 0, 4), after(x, 2, 4)
+    push(keyval_in, mine, KV_Z_NEAR, {"z_hi": z_up})
+    push(keyval_in, mine, KV_Z_NEAR + 1, {"z_hi": z_down})
+    keep(keyval_in, mine, KV_Z_NEAR)
     wait_bytes(w_out_all.at[0, pl.ds(0, 1)], local.at[OUT_Z])
     wait_bytes(w_out_all.at[0, pl.ds(0, 3)], recv.at[OUT_Z])
     quad = w_out_all.at[core, pl.ds(y * 4, 4)]
@@ -238,30 +240,46 @@
         return jnp.concatenate(pieces, axis=-1).reshape(128, 256)
 
     up, down = after(y, 0, 4), after(y, 2, 4)
+
+    def origin(step):
+        return lax.rem(z_hi + 3 - step, 4)
+
     for step in range(4):
         if step == 3:
             wait_bytes(left_z.at[pl.ds(0, 1)], local.at[LEFT_QUARTER + step])
         wait_bytes(left_z.at[pl.ds(0, 3 if step == 3 else 4)], recv.at[LEFT_QUARTER + step])
-        source = lax.rem(z_hi + 3 - step, 4)
+        over_x(left_z, left_x, LEFT_X, step, origin(step))
+    for step in range(4):
+        end_x(left_x, LEFT_X, step)
+        source = origin(step)
         for part in range(2):
-            left_all[y, source, :, part * 128 : part * 128 + 128] = tiles(left_z, source, part).T
+            left_all[y, source, :, part * 128 : part * 128 + 128] = tiles(left_x, source, part).T
         own = left_all.at[y, source]
         push(own, own, LEFT_UP + step, {"y": up})
         push(own, own, LEFT_DOWN + step, {"y": down})
     for step in range(4):
-        source = lax.rem(z_hi + 3 - step, 4)
+        source = origin(step)
         wait_bytes(left_all.at[y, 0], recv.at[LEFT_UP + step])
         passed = left_all.at[down, source, pl.ds(0, 128)]
         push(passed, passed, LEFT_FAR, {"y": up})
         wait_bytes(left_all.at[y, 0], recv.at[LEFT_DOWN + step])
         passed = left_all.at[up, source, pl.ds(128, 128)]
         push(passed, passed, LEFT_FAR + 1, {"y": down})
+    wait_bytes(keyval_in, local.at[KV_Z_NEAR])
+    wait_bytes(keyval_in, recv.at[KV_Z_NEAR])
+    wait_bytes(keyval_in, recv.at[KV_Z_NEAR + 1])
+
+    def over_x_ring(part):
+        block = keyval.at[part * 4 + x, core]
+        push(block, block, KV_X_NEAR, {"x": x_up})
+        push(block, block, KV_X_NEAR + 1, {"x": x_down})
+
+    each(3, lambda step: over_x_ring(lax.rem(z_hi + 3 + step, 4)))
     end_z(right_z, RIGHT_Z)
-    mine = keyval.at[z_hi * 4 + x, core]
-    z_up, z_down, x_up, x_down = after(z_hi, 0, 4), after(z_hi, 2, 4), after(x, 0, 4), after(x, 2, 4)
-    push(keyval_in, mine, KV_Z_NEAR, {"z_hi": z_up})
-    push(keyval_in, mine, KV_Z_NEAR + 1, {"z_hi": z_down})
-    keep(keyval_in, mine, KV_Z_NEAR)
+    passed = keyval.at[z_down * 4 + x, core, pl.ds(0, 2)]
+    push(passed, passed, KV_Z_FAR, {"z_hi": z_up})
+    passed = keyval.at[z_up * 4 + x, core, pl.ds(2, 2)]
+    push(passed, passed, KV_Z_FAR + 1, {"z_hi": z_down})
     for z_part in range(4):
         for part in range(2):
             first = z_part * 256 + part * 128
@@ -279,24 +297,10 @@
             sums[part * 4 + low] = jnp.concatenate(
                 [product[:, 0, :, cut], product[:, 1, :, cut]], axis=-1
             )
-        over_x(sums, sums_x, SUM_X, step)
+        over_x(sums, sums_x, SUM_X, step, part)
     for step in range(4):
         end_x(sums_x, SUM_X, step)
         over_z(sums_x, tri, SUM_Z, step)
-    wait_bytes(keyval_in, local.at[KV_Z_NEAR])
-    wait_bytes(keyval_in, recv.at[KV_Z_NEAR])
-    passed = keyval.at[z_down * 4 + x, core, pl.ds(0, 2)]
-    push(passed, passed, KV_Z_FAR, {"z_hi": z_up})
-    wait_bytes(keyval_in, recv.at[KV_Z_NEAR + 1])
-    passed = keyval.at[z_up * 4 + x, core, pl.ds(2, 2)]
-    push(passed, passed, KV_Z_FAR + 1, {"z_hi": z_down})
-
-    def over_x_ring(part):
-        block = keyval.at[part * 4 + x, core]
-        push(block, block, KV_X_NEAR, {"x": x_up})
-        push(block, block, KV_X_NEAR + 1, {"x": x_down})
-
-    each(3, lambda step: over_x_ring(lax.rem(z_hi + 3 + step, 4)))
     wait_bytes(w_out_all.at[0, pl.ds(0, 12)], recv.at[OUT_Y])
     push(w_out_all.at[core], w_out_all.at[core], OUT_CORE, {"core": 1 - core})
     wait_bytes(keyval_in.at[pl.ds(0, 2)], recv.at[KV_Z_FAR])

time: 147 us -> 133 us (0.905)
  Pallas kernels: 142 us -> 128 us
    pallas_call x1, Pallas kernels: 142 us -> 128 us  [per_device(): pl.pallas_call(whole_kernel, out_shape=(jax.ShapeDtypeStruct((2048, 128),...]
where the time goes in v5:
time: 133 us; the launch traced here: 132 us
  Pallas kernels  128 us (96%)
  local copies, waits for them, and re-layouts  3.33 us (3%)
    pallas_call x1, Pallas kernels, per_device(): pl.pallas_call(whole_kernel, out_shape=(jax.ShapeDtypeStruct((2048, 128),...  128 us
    unnamed x7, local copies, waits for them, and re-layouts  3.33 us

profile of v5, /device:TPU:6, one launch (start us, length us, event | category | flops | bytes accessed | tf_op | source)
XLA Modules:
  0.0 131.5 jit_solution(6794025445003055387)
XLA Ops:
  0.6 127.5 %whole.1 = (bf16[2048,128]{1,0:T(8,128)(2,1)}, bf16[4,32,1024]{2,1,0:T(8,128)(2,1)}, bf16[32,768]{1,0:T(8,128)(2,1)}) custom-call(bf16[2048,128]{1,0:T(8,128)(2,1)} %bitcast.14, s32[1,1024]{1,0:T(1,128)} %bitcast.19, bf16[128,640]{1,0:T(8,128)(2,1)} %w_tri_in_h.1, bf16[128,128]{1,0:T(8,128)(2,1)} %w_tri_out_h.1, bf16[64,128]{1,0:T(8,128)(2,1)} %bitcast.18, ...), custom_call_target="tpu_custom_call" | custom-call | tf_op jit(solution)/shard_map/whole/pallas_call | solution.py:437
  128.2 0.0 copy-start
  128.2 1.9 %copy.15 = bf16[32,64,128]{2,1,0:T(8,128)(2,1)} copy(bf16[32,64,128]{2,1,0:T(8,128)(2,1)} %bitcast.13) | data formatting | bytes 1048576
  130.1 0.0 copy-done
  130.1 0.0 copy-start.1
  130.1 0.7 copy.16
  130.8 0.1 copy-done.1
  130.9 0.6 copy.17
Async XLA Ops:
  128.2 1.9 %copy-start = (bf16[4,32,1024]{2,1,0:T(8,128)(2,1)S(1)}, bf16[4,32,1024]{2,1,0:T(8,128)(2,1)}, u32[]{:S(2)}) copy-start(bf16[4,32,1024]{2,1,0:T(8,128)(2,1)} %get-tuple-element.7) | copy-start | bytes 786436
  130.1 0.8 copy-start.1

commit v6 on v5

--- a/solution.py
+++ b/solution.py
@@ -16,12 +16,12 @@
 F32 = jnp.float32
 
 LEFT_X, RIGHT_X, SUM_X = 0, 4, 8
-RIGHT_Z, SUM_Z = 13, 14
+SUM_Z = 14
 OUT_Z, OUT_Y, OUT_CORE, KV_CORE = 15, 16, 17, 18
 BIAS_FIRST, BIAS_REST, HEADS_OUT = 19, 20, 21
 LEFT_FAR, KV_Z_NEAR, KV_Z_FAR, KV_X_NEAR, KV_X_FAR = 22, 24, 26, 28, 30
-LEFT_UP, LEFT_DOWN, LEFT_QUARTER = 32, 36, 40
-SLOTS = 44
+LEFT_UP, LEFT_DOWN, LEFT_QUARTER, RIGHT_QUARTER = 32, 36, 40, 44
+SLOTS = 48
 
 
 def block_of(index):
@@ -53,13 +53,13 @@
 
 def whole_kernel(
     pair_h, mask_h, w_tri_in_h, w_tri_out_h, w_bias_h, single_h, w_attn_h, w_out_h,
-    new_pair, biases, attended,
+    new_pair_h, biases, attended,
     pair, mask, w_tri_in, w_tri_out, w_bias, single, w_attn, w_out,
     left_in, right_in, left_x, right_x, left_z, right_z, sums, sums_x, tri,
     gather_in, own_in,
-    left_all, right_own, keyval, keyval_in, w_out_all,
+    left_all, totals, keyval, keyval_in, w_out_all,
     normed, gate, rows_f, w_in_t, query, agate, score, bias_f, probs,
-    bias_in, bias_all, heads_in, heads_all,
+    bias_in, bias_all, heads_in, heads_all, new_pair,
     send, recv, local, load,
 ):
     z_hi, z_lo = lax.axis_index("z_hi"), lax.axis_index("z_lo")
@@ -162,28 +162,44 @@
 
     w_in_t[...] = w_tri_in[:, 0:512].T
 
-    def factor(block, first):
+    def factor(block, first, half):
         rows = slice(block * 256, block * 256 + 256)
-        both = contract_last(w_in_t[first : first + 256, :], normed[rows, :])
-        value = jax.nn.sigmoid(both[128:]) * both[:128]
-        for half in range(2):
-            line = block * 2 + half
-            part = value[:, half * 128 : half * 128 + 128] * cell_mask[line : line + 1]
-            rows_f[pl.ds(line, 128, stride=16), :] = part
-
-    for block in range(8):
-        rows = slice(block * 256, block * 256 + 256)
-        normed[rows, :] = layer_norm(pair[rows, :].astype(F32), 1).astype(BF16)
-        factor(block, 0)
-    left_in[...] = rows_f[...].astype(BF16).reshape(16, 8, 16, 128)
-    pl.semaphore_wait(barrier, 37)
-    for step in range(4):
-        over_z(left_in, left_z, LEFT_QUARTER + step, step)
-    for block in range(8):
-        factor(block, 256)
-    right_in[...] = rows_f[...].astype(BF16).reshape(16, 8, 16, 128)
-    for step in range(4):
-        over_x(right_in, right_x, RIGHT_X, step, quarter(step))
+        parts = (quarter(half * 2), quarter(half * 2 + 1))
+        weights = [
+            w_in_t[pl.ds(pl.multiple_of(start + part * 32, 32), 32), :]
+            for start in (first, first + 128)
+            for part in parts
+        ]
+        both = contract_last(jnp.concatenate(weights, axis=0), normed[rows, :])
+        value = jax.nn.sigmoid(both[64:]) * both[:64]
+        for side in range(2):
+            line = block * 2 + side
+            masked = value[:, side * 128 : side * 128 + 128] * cell_mask[line : line + 1]
+            for place, part in enumerate(parts):
+                rows_f[pl.ds(part * 512 + line, 32, stride=16), :] = masked[place * 32 : place * 32 + 32]
+
+    def rounded(dst, step):
+        part = quarter(step)
+        lines = rows_f[pl.ds(pl.multiple_of(part * 512, 512), 512), :]
+        dst[pl.ds(part * 4, 4)] = lines.astype(BF16).reshape(4, 8, 16, 128)
+
+    for half in range(2):
+        for block in range(8):
+            if half == 0:
+                rows = slice(block * 256, block * 256 + 256)
+                normed[rows, :] = layer_norm(pair[rows, :].astype(F32), 1).astype(BF16)
+            factor(block, 0, half)
+        if half == 0:
+            pl.semaphore_wait(barrier, 37)
+        for step in (half * 2, half * 2 + 1):
+            rounded(left_in, step)
+            over_z(left_in, left_z, LEFT_QUARTER + step, step)
+    for half in range(2):
+        for block in range(8):
+            factor(block, 256, half)
+        for step in (half * 2, half * 2 + 1):
+            rounded(right_in, step)
+            over_x(right_in, right_x, RIGHT_X, step, quarter(step))
     loads[3].wait()
     half_out = w_out.at[:, pl.ds(pl.multiple_of(core * 384, 128), 384)]
     each(3, lambda step: push(half_out, w_out_all.at[core, head], OUT_Z, near("z_lo", z_lo, step, 4)))
@@ -221,7 +237,7 @@
     for step in range(4):
         end_x(right_x, RIGHT_X, step)
         sent_z(LEFT_QUARTER, step)
-        over_z(right_x, right_z, RIGHT_Z, step)
+        over_z(right_x, right_z, RIGHT_QUARTER + step, step)
     mine = keyval.at[z_hi * 4 + x, core]
     z_up, z_down, x_up, x_down = after(z_hi, 0, 4), after(z_hi, 2, 4), after(x, 0, 4), after(x, 2, 4)
     push(keyval_in, mine, KV_Z_NEAR, {"z_hi": z_up})
@@ -244,10 +260,13 @@
     def origin(step):
         return lax.rem(z_hi + 3 - step, 4)
 
-    for step in range(4):
+    def end_quarter(slot, step):
         if step == 3:
-            wait_bytes(left_z.at[pl.ds(0, 1)], local.at[LEFT_QUARTER + step])
-        wait_bytes(left_z.at[pl.ds(0, 3 if step == 3 else 4)], recv.at[LEFT_QUARTER + step])
+            wait_bytes(left_z.at[pl.ds(0, 1)], local.at[slot + step])
+        wait_bytes(left_z.at[pl.ds(0, 3 if step == 3 else 4)], recv.at[slot + step])
+
+    for step in range(4):
+        end_quarter(LEFT_QUARTER, step)
         over_x(left_z, left_x, LEFT_X, step, origin(step))
     for step in range(4):
         end_x(left_x, LEFT_X, step)
@@ -265,39 +284,42 @@
         wait_bytes(left_all.at[y, 0], recv.at[LEFT_DOWN + step])
         passed = left_all.at[up, source, pl.ds(128, 128)]
         push(passed, passed, LEFT_FAR + 1, {"y": down})
-    wait_bytes(keyval_in, local.at[KV_Z_NEAR])
-    wait_bytes(keyval_in, recv.at[KV_Z_NEAR])
-    wait_bytes(keyval_in, recv.at[KV_Z_NEAR + 1])
-
     def over_x_ring(part):
         block = keyval.at[part * 4 + x, core]
         push(block, block, KV_X_NEAR, {"x": x_up})
         push(block, block, KV_X_NEAR + 1, {"x": x_down})
 
-    each(3, lambda step: over_x_ring(lax.rem(z_hi + 3 + step, 4)))
-    end_z(right_z, RIGHT_Z)
-    passed = keyval.at[z_down * 4 + x, core, pl.ds(0, 2)]
-    push(passed, passed, KV_Z_FAR, {"z_hi": z_up})
-    passed = keyval.at[z_up * 4 + x, core, pl.ds(2, 2)]
-    push(passed, passed, KV_Z_FAR + 1, {"z_hi": z_down})
-    for z_part in range(4):
-        for part in range(2):
-            first = z_part * 256 + part * 128
-            right_own[first : first + 128, :] = tiles(right_z, z_part, part)
     for way in range(2):
         wait_bytes(left_all.at[0, pl.ds(0, 2)], recv.at[LEFT_FAR + way])
     for step in range(4):
-        part = quarter(step)
-        product = sum(
-            matmul(left_all[part, quad], right_own[quad * 256 : quad * 256 + 256]) for quad in range(4)
-        )
-        product = product.astype(BF16).reshape(8, 2, 16, 256)
-        for low in range(4):
-            cut = slice(low * 64, low * 64 + 64)
-            sums[part * 4 + low] = jnp.concatenate(
-                [product[:, 0, :, cut], product[:, 1, :, cut]], axis=-1
-            )
-        over_x(sums, sums_x, SUM_X, step, part)
+        if step == 3:
+            wait_bytes(keyval_in, local.at[KV_Z_NEAR])
+            wait_bytes(keyval_in, recv.at[KV_Z_NEAR])
+            wait_bytes(keyval_in, recv.at[KV_Z_NEAR + 1])
+            each(3, lambda step: over_x_ring(lax.rem(z_hi + 3 + step, 4)))
+        end_quarter(RIGHT_QUARTER, step)
+        if step == 3:
+            passed = keyval.at[z_down * 4 + x, core, pl.ds(0, 2)]
+            push(passed, passed, KV_Z_FAR, {"z_hi": z_up})
+            passed = keyval.at[z_up * 4 + x, core, pl.ds(2, 2)]
+            push(passed, passed, KV_Z_FAR + 1, {"z_hi": z_down})
+        source = origin(step)
+        block = jnp.concatenate([tiles(right_z, source, part) for part in range(2)], axis=0)
+        for turn in range(4):
+            part = quarter(turn)
+            product = matmul(left_all[part, source], block)
+            if step > 0:
+                product += totals[turn]
+            if step < 3:
+                totals[turn] = product
+                continue
+            product = product.astype(BF16).reshape(8, 2, 16, 256)
+            for low in range(4):
+                cut = slice(low * 64, low * 64 + 64)
+                sums[part * 4 + low] = jnp.concatenate(
+                    [product[:, 0, :, cut], product[:, 1, :, cut]], axis=-1
+                )
+            over_x(sums, sums_x, SUM_X, turn, part)
     for step in range(4):
         end_x(sums_x, SUM_X, step)
         over_z(sums_x, tri, SUM_Z, step)
@@ -341,7 +363,6 @@
         for half in range(2):
             rows = pl.ds(block * 2 + half, 64, stride=16)
             bias_f[rows, :] = bias[:, half * 128 : half * 128 + 128]
-    bias_in[...] = bias_f[...].astype(BF16).reshape(4, 16, 16, 128)
 
     def send_bias(layers, slot):
         def body(step):
@@ -351,8 +372,12 @@
         each(15, body)
         keep(bias_in.at[layers, head], bias_all.at[layers, head], slot)
 
+    bias_in[0] = bias_f[0:256, :].astype(BF16).reshape(16, 16, 128)
     send_bias(pl.ds(0, 1), BIAS_FIRST)
+    bias_in[1:4] = bias_f[256:1024, :].astype(BF16).reshape(3, 16, 16, 128)
     send_bias(pl.ds(1, 3), BIAS_REST)
+    store = pltpu.make_async_copy(new_pair, new_pair_h, load.at[8])
+    store.start()
     wait_bytes(keyval.at[:, 0], recv.at[KV_CORE])
     for group in range(2):
         rows = slice(group * 256, group * 256 + 256)
@@ -409,11 +434,13 @@
         weights = w_out_all[half].reshape(HEADS * HEAD_DIM, 384)
         attended[:, half * 384 : half * 384 + 384] = matmul(merged, weights).astype(BF16)
 
+    store.wait()
     for slot in (LEFT_X, RIGHT_X, SUM_X):
         for step in range(4):
             wait_bytes(left_x.at[pl.ds(0, 4), pl.ds(0, 7)], send.at[slot + step])
-    for slot in (RIGHT_Z, SUM_Z):
-        wait_bytes(left_z.at[pl.ds(0, 15)], send.at[slot])
+    for step in range(4):
+        sent_z(RIGHT_QUARTER, step)
+    wait_bytes(left_z.at[pl.ds(0, 15)], send.at[SUM_Z])
     for way in range(2):
         for step in range(4):
             wait_bytes(left_all.at[0, 0], send.at[(LEFT_UP, LEFT_DOWN)[way] + step])
@@ -442,7 +469,7 @@
             jax.ShapeDtypeStruct((32, 768), BF16),
         ),
         in_specs=[pl.BlockSpec(memory_space=pltpu.HBM)] * 8,
-        out_specs=(vmem, vmem, vmem),
+        out_specs=(pl.BlockSpec(memory_space=pltpu.HBM), vmem, vmem),
         scratch_shapes=[
             pltpu.VMEM((2048, 128), BF16),
             pltpu.VMEM((1, 1024), jnp.int32),
@@ -458,7 +485,7 @@
             pltpu.VMEM((WIDE, 128), BF16),
             pltpu.VMEM((256, WIDE), F32),
             pltpu.VMEM((4, 4, 256, 256), BF16),
-            pltpu.VMEM((1024, 256), BF16),
+            pltpu.VMEM((4, 256, 256), F32),
             pltpu.VMEM((16, 2, 4, 32, WIDE), BF16),
             pltpu.VMEM((4, 32, WIDE), BF16),
             pltpu.VMEM((2, HEADS, HEAD_DIM, 384), BF16),
@@ -475,10 +502,11 @@
             pltpu.VMEM((LAYERS, 16, 16, 128), BF16),
             pltpu.VMEM((16, 32, 128), BF16),
             pltpu.VMEM((16, 32, 128), BF16),
+            pltpu.VMEM((2048, 128), BF16),
             pltpu.SemaphoreType.DMA((SLOTS,)),
             pltpu.SemaphoreType.DMA((SLOTS,)),
             pltpu.SemaphoreType.DMA((SLOTS,)),
-            pltpu.SemaphoreType.DMA((8,)),
+            pltpu.SemaphoreType.DMA((9,)),
         ],
         compiler_params=pltpu.CompilerParams(
             collective_id=0, has_side_effects=True, vmem_limit_bytes=60 * 1024 * 1024

time: 133 us -> 139 us (1.045); the launches traced: 132 us -> 139 us
  Pallas kernels: 128 us -> 135 us
    pallas_call x1, Pallas kernels: 128 us -> 135 us  [per_device(): pl.pallas_call(whole_kernel, out_shape=(jax.ShapeDtypeStruct((2048, 128),...]
where the time goes in v6:
time: 139 us
  Pallas kernels  135 us (97%)
  local copies, waits for them, and re-layouts  3.33 us (2%)
    pallas_call x1, Pallas kernels, per_device(): pl.pallas_call(whole_kernel, out_shape=(jax.ShapeDtypeStruct((2048, 128),...  135 us
    unnamed x7, local copies, waits for them, and re-layouts  3.33 us

profile of v6, /device:TPU:6, one launch (start us, length us, event | category | flops | bytes accessed | tf_op | source)
XLA Modules:
  0.0 139.1 jit_solution(14660860353205005732)
XLA Ops:
  0.6 135.1 %whole.1 = (bf16[2048,128]{1,0:T(8,128)(2,1)}, bf16[4,32,1024]{2,1,0:T(8,128)(2,1)}, bf16[32,768]{1,0:T(8,128)(2,1)}) custom-call(bf16[2048,128]{1,0:T(8,128)(2,1)} %bitcast.14, s32[1,1024]{1,0:T(1,128)} %bitcast.19, bf16[128,640]{1,0:T(8,128)(2,1)} %w_tri_in_h.1, bf16[128,128]{1,0:T(8,128)(2,1)} %w_tri_out_h.1, bf16[64,128]{1,0:T(8,128)(2,1)} %bitcast.18, ...), custom_call_target="tpu_custom_call" | custom-call | tf_op jit(solution)/shard_map/whole/pallas_call | solution.py:464
  135.7 0.0 copy-start
  135.7 1.9 %copy.15 = bf16[32,64,128]{2,1,0:T(8,128)(2,1)} copy(bf16[32,64,128]{2,1,0:T(8,128)(2,1)} %bitcast.13) | data formatting | bytes 1048576
  137.7 0.0 copy-done
  137.7 0.0 copy-start.1
  137.7 0.7 copy.16
  138.4 0.1 copy-done.1
  138.5 0.6 copy.17
Async XLA Ops:
  135.7 1.9 %copy-start = (bf16[4,32,1024]{2,1,0:T(8,128)(2,1)S(1)}, bf16[4,32,1024]{2,1,0:T(8,128)(2,1)}, u32[]{:S(2)}) copy-start(bf16[4,32,1024]{2,1,0:T(8,128)(2,1)} %get-tuple-element.7) | copy-start | bytes 786436
  137.7 0.8 copy-start.1

commit v7 on v6

--- a/solution.py
+++ b/solution.py
@@ -162,44 +162,28 @@
 
     w_in_t[...] = w_tri_in[:, 0:512].T
 
-    def factor(block, first, half):
+    def factor(block, first):
         rows = slice(block * 256, block * 256 + 256)
-        parts = (quarter(half * 2), quarter(half * 2 + 1))
-        weights = [
-            w_in_t[pl.ds(pl.multiple_of(start + part * 32, 32), 32), :]
-            for start in (first, first + 128)
-            for part in parts
-        ]
-        both = contract_last(jnp.concatenate(weights, axis=0), normed[rows, :])
-        value = jax.nn.sigmoid(both[64:]) * both[:64]
-        for side in range(2):
-            line = block * 2 + side
-            masked = value[:, side * 128 : side * 128 + 128] * cell_mask[line : line + 1]
-            for place, part in enumerate(parts):
-                rows_f[pl.ds(part * 512 + line, 32, stride=16), :] = masked[place * 32 : place * 32 + 32]
-
-    def rounded(dst, step):
-        part = quarter(step)
-        lines = rows_f[pl.ds(pl.multiple_of(part * 512, 512), 512), :]
-        dst[pl.ds(part * 4, 4)] = lines.astype(BF16).reshape(4, 8, 16, 128)
-
-    for half in range(2):
-        for block in range(8):
-            if half == 0:
-                rows = slice(block * 256, block * 256 + 256)
-                normed[rows, :] = layer_norm(pair[rows, :].astype(F32), 1).astype(BF16)
-            factor(block, 0, half)
-        if half == 0:
-            pl.semaphore_wait(barrier, 37)
-        for step in (half * 2, half * 2 + 1):
-            rounded(left_in, step)
-            over_z(left_in, left_z, LEFT_QUARTER + step, step)
-    for half in range(2):
-        for block in range(8):
-            factor(block, 256, half)
-        for step in (half * 2, half * 2 + 1):
-            rounded(right_in, step)
-            over_x(right_in, right_x, RIGHT_X, step, quarter(step))
+        both = contract_last(w_in_t[first : first + 256, :], normed[rows, :])
+        value = jax.nn.sigmoid(both[128:]) * both[:128]
+        for half in range(2):
+            line = block * 2 + half
+            part = value[:, half * 128 : half * 128 + 128] * cell_mask[line : line + 1]
+            rows_f[pl.ds(line, 128, stride=16), :] = part
+
+    for block in range(8):
+        rows = slice(block * 256, block * 256 + 256)
+        normed[rows, :] = layer_norm(pair[rows, :].astype(F32), 1).astype(BF16)
+        factor(block, 0)
+    left_in[...] = rows_f[...].astype(BF16).reshape(16, 8, 16, 128)
+    pl.semaphore_wait(barrier, 37)
+    for step in range(4):
+        over_z(left_in, left_z, LEFT_QUARTER + step, step)
+    for block in range(8):
+        factor(block, 256)
+    right_in[...] = rows_f[...].astype(BF16).reshape(16, 8, 16, 128)
+    for step in range(4):
+        over_x(right_in, right_x, RIGHT_X, step, quarter(step))
     loads[3].wait()
     half_out = w_out.at[:, pl.ds(pl.multiple_of(core * 384, 128), 384)]
     each(3, lambda step: push(half_out, w_out_all.at[core, head], OUT_Z, near("z_lo", z_lo, step, 4)))

time: 139 us -> 139 us (level)
  no operation moved by 1% of the time
where the time goes in v7:
time: 139 us
  Pallas kernels  135 us (97%)
  local copies, waits for them, and re-layouts  3.33 us (2%)
    pallas_call x1, Pallas kernels, per_device(): pl.pallas_call(whole_kernel, out_shape=(jax.ShapeDtypeStruct((2048, 128),...  135 us
    unnamed x7, local copies, waits for them, and re-layouts  3.33 us

profile of v7, /device:TPU:6, one launch (start us, length us, event | category | flops | bytes accessed | tf_op | source)
XLA Modules:
  0.0 139.0 jit_solution(2875964104670320909)
XLA Ops:
  0.6 135.0 %whole.1 = (bf16[2048,128]{1,0:T(8,128)(2,1)}, bf16[4,32,1024]{2,1,0:T(8,128)(2,1)}, bf16[32,768]{1,0:T(8,128)(2,1)}) custom-call(bf16[2048,128]{1,0:T(8,128)(2,1)} %bitcast.14, s32[1,1024]{1,0:T(1,128)} %bitcast.19, bf16[128,640]{1,0:T(8,128)(2,1)} %w_tri_in_h.1, bf16[128,128]{1,0:T(8,128)(2,1)} %w_tri_out_h.1, bf16[64,128]{1,0:T(8,128)(2,1)} %bitcast.18, ...), custom_call_target="tpu_custom_call" | custom-call | tf_op jit(solution)/shard_map/whole/pallas_call | solution.py:448
  135.6 0.0 copy-start
  135.6 1.9 %copy.15 = bf16[32,64,128]{2,1,0:T(8,128)(2,1)} copy(bf16[32,64,128]{2,1,0:T(8,128)(2,1)} %bitcast.13) | data formatting | bytes 1048576
  137.6 0.0 copy-done
  137.6 0.0 copy-start.1
  137.6 0.7 copy.16
  138.3 0.1 copy-done.1
  138.4 0.6 copy.17
Async XLA Ops:
  135.6 1.9 %copy-start = (bf16[4,32,1024]{2,1,0:T(8,128)(2,1)S(1)}, bf16[4,32,1024]{2,1,0:T(8,128)(2,1)}, u32[]{:S(2)}) copy-start(bf16[4,32,1024]{2,1,0:T(8,128)(2,1)} %get-tuple-element.7) | copy-start | bytes 786436
  137.6 0.8 copy-start.1

commit v8 on v7

--- a/solution.py
+++ b/solution.py
@@ -57,7 +57,7 @@
     pair, mask, w_tri_in, w_tri_out, w_bias, single, w_attn, w_out,
     left_in, right_in, left_x, right_x, left_z, right_z, sums, sums_x, tri,
     gather_in, own_in,
-    left_all, totals, keyval, keyval_in, w_out_all,
+    left_all, right_own, keyval, keyval_in, w_out_all,
     normed, gate, rows_f, w_in_t, query, agate, score, bias_f, probs,
     bias_in, bias_all, heads_in, heads_all, new_pair,
     send, recv, local, load,
@@ -273,14 +273,11 @@
         push(block, block, KV_X_NEAR, {"x": x_up})
         push(block, block, KV_X_NEAR + 1, {"x": x_down})
 
-    for way in range(2):
-        wait_bytes(left_all.at[0, pl.ds(0, 2)], recv.at[LEFT_FAR + way])
-    for step in range(4):
-        if step == 3:
-            wait_bytes(keyval_in, local.at[KV_Z_NEAR])
-            wait_bytes(keyval_in, recv.at[KV_Z_NEAR])
-            wait_bytes(keyval_in, recv.at[KV_Z_NEAR + 1])
-            each(3, lambda step: over_x_ring(lax.rem(z_hi + 3 + step, 4)))
+    wait_bytes(keyval_in, local.at[KV_Z_NEAR])
+    wait_bytes(keyval_in, recv.at[KV_Z_NEAR])
+    wait_bytes(keyval_in, recv.at[KV_Z_NEAR + 1])
+    each(3, lambda step: over_x_ring(lax.rem(z_hi + 3 + step, 4)))
+    for step in range(4):
         end_quarter(RIGHT_QUARTER, step)
         if step == 3:
             passed = keyval.at[z_down * 4 + x, core, pl.ds(0, 2)]
@@ -288,22 +285,20 @@
             passed = keyval.at[z_up * 4 + x, core, pl.ds(2, 2)]
             push(passed, passed, KV_Z_FAR + 1, {"z_hi": z_down})
         source = origin(step)
-        block = jnp.concatenate([tiles(right_z, source, part) for part in range(2)], axis=0)
-        for turn in range(4):
-            part = quarter(turn)
-            product = matmul(left_all[part, source], block)
-            if step > 0:
-                product += totals[turn]
-            if step < 3:
-                totals[turn] = product
-                continue
-            product = product.astype(BF16).reshape(8, 2, 16, 256)
-            for low in range(4):
-                cut = slice(low * 64, low * 64 + 64)
-                sums[part * 4 + low] = jnp.concatenate(
-                    [product[:, 0, :, cut], product[:, 1, :, cut]], axis=-1
-                )
-            over_x(sums, sums_x, SUM_X, turn, part)
+        for part in range(2):
+            right_own[source, part * 128 : part * 128 + 128, :] = tiles(right_z, source, part)
+    for way in range(2):
+        wait_bytes(left_all.at[0, pl.ds(0, 2)], recv.at[LEFT_FAR + way])
+    for step in range(4):
+        part = quarter(step)
+        product = sum(matmul(left_all[part, quad], right_own[quad]) for quad in range(4))
+        product = product.astype(BF16).reshape(8, 2, 16, 256)
+        for low in range(4):
+            cut = slice(low * 64, low * 64 + 64)
+            sums[part * 4 + low] = jnp.concatenate(
+                [product[:, 0, :, cut], product[:, 1, :, cut]], axis=-1
+            )
+        over_x(sums, sums_x, SUM_X, step, part)
     for step in range(4):
         end_x(sums_x, SUM_X, step)
         over_z(sums_x, tri, SUM_Z, step)
@@ -469,7 +464,7 @@
             pltpu.VMEM((WIDE, 128), BF16),
             pltpu.VMEM((256, WIDE), F32),
             pltpu.VMEM((4, 4, 256, 256), BF16),
-            pltpu.VMEM((4, 256, 256), F32),
+            pltpu.VMEM((4, 256, 256), BF16),
             pltpu.VMEM((16, 2, 4, 32, WIDE), BF16),
             pltpu.VMEM((4, 32, WIDE), BF16),
             pltpu.VMEM((2, HEADS, HEAD_DIM, 384), BF16),

time: 139 us -> 133 us (0.957); the launches traced: 139 us -> 131 us
  Pallas kernels: 135 us -> 127 us
    pallas_call x1, Pallas kernels: 135 us -> 127 us  [per_device(): pl.pallas_call(whole_kernel, out_shape=(jax.ShapeDtypeStruct((2048, 128),...]
where the time goes in v8:
time: 133 us; the launch traced here: 131 us
  Pallas kernels  127 us (95%)
  local copies, waits for them, and re-layouts  3.33 us (3%)
    pallas_call x1, Pallas kernels, per_device(): pl.pallas_call(whole_kernel, out_shape=(jax.ShapeDtypeStruct((2048, 128),...  127 us
    unnamed x7, local copies, waits for them, and re-layouts  3.33 us

profile of v8, /device:TPU:6, one launch (start us, length us, event | category | flops | bytes accessed | tf_op | source)
XLA Modules:
  0.0 131.5 jit_solution(1987131925792191314)
XLA Ops:
  0.6 127.5 %whole.1 = (bf16[2048,128]{1,0:T(8,128)(2,1)}, bf16[4,32,1024]{2,1,0:T(8,128)(2,1)}, bf16[32,768]{1,0:T(8,128)(2,1)}) custom-call(bf16[2048,128]{1,0:T(8,128)(2,1)} %bitcast.14, s32[1,1024]{1,0:T(1,128)} %bitcast.19, bf16[128,640]{1,0:T(8,128)(2,1)} %w_tri_in_h.1, bf16[128,128]{1,0:T(8,128)(2,1)} %w_tri_out_h.1, bf16[64,128]{1,0:T(8,128)(2,1)} %bitcast.18, ...), custom_call_target="tpu_custom_call" | custom-call | tf_op jit(solution)/shard_map/whole/pallas_call | solution.py:443
  128.1 0.0 copy-start
  128.1 1.9 %copy.15 = bf16[32,64,128]{2,1,0:T(8,128)(2,1)} copy(bf16[32,64,128]{2,1,0:T(8,128)(2,1)} %bitcast.13) | data formatting | bytes 1048576
  130.0 0.0 copy-done
  130.0 0.0 copy-start.1
  130.0 0.7 copy.16
  130.7 0.1 copy-done.1
  130.8 0.6 copy.17
Async XLA Ops:
  128.1 1.9 %copy-start = (bf16[4,32,1024]{2,1,0:T(8,128)(2,1)S(1)}, bf16[4,32,1024]{2,1,0:T(8,128)(2,1)}, u32[]{:S(2)}) copy-start(bf16[4,32,1024]{2,1,0:T(8,128)(2,1)} %get-tuple-element.7) | copy-start | bytes 786436
  130.0 0.8 copy-start.1

commit v9 on v8

--- a/solution.py
+++ b/solution.py
@@ -56,7 +56,7 @@
     new_pair_h, biases, attended,
     pair, mask, w_tri_in, w_tri_out, w_bias, single, w_attn, w_out,
     left_in, right_in, left_x, right_x, left_z, right_z, sums, sums_x, tri,
-    gather_in, own_in,
+    gather_in, own_in, xn, projected,
     left_all, right_own, keyval, keyval_in, w_out_all,
     normed, gate, rows_f, w_in_t, query, agate, score, bias_f, probs,
     bias_in, bias_all, heads_in, heads_all, new_pair,
@@ -85,8 +85,8 @@
         pltpu.make_async_copy(src, dst, load.at[slot])
         for slot, (src, dst) in enumerate(
             (
-                (pair_h, pair), (w_tri_in_h, w_tri_in), (mask_h, mask), (w_out_h, w_out),
-                (w_attn_h, w_attn), (single_h, single), (w_tri_out_h, w_tri_out), (w_bias_h, w_bias),
+                (single_h, single), (w_attn_h, w_attn), (pair_h, pair), (w_tri_in_h, w_tri_in),
+                (mask_h, mask), (w_out_h, w_out), (w_tri_out_h, w_tri_out), (w_bias_h, w_bias),
             )
         )
     ]
@@ -145,7 +145,39 @@
         wait_bytes(dst.at[pl.ds(0, 1)], local.at[slot])
         wait_bytes(dst.at[pl.ds(0, 15)], recv.at[slot])
 
-    for copy in loads[:3]:
+    head_lane = lax.broadcasted_iota(jnp.int32, (1, WIDE), 1)
+    head_block = block_of(head_lane)
+    place = lax.broadcasted_iota(jnp.int32, (256, WIDE), 0)
+    own_in[...] = ((place >= 32 * head_block) & (place < 32 * head_block + 32)).astype(F32)
+
+    def spread(first, count):
+        place = lax.broadcasted_iota(jnp.int32, (4 * HEAD_DIM, WIDE), 0)
+        source = head_lane - HEAD_DIM * head_block
+        parts = [
+            (place == source + HEAD_DIM * (first + n)).astype(F32).astype(BF16) for n in range(count)
+        ]
+        return jnp.concatenate(parts, axis=1) if count > 1 else parts[0]
+
+    for copy in loads[:2]:
+        copy.wait()
+    key_value = spread(1, 2)
+    for group in range(2):
+        rows = slice(group * 256, group * 256 + 256)
+        xn[rows, :] = layer_norm(single[rows, :].astype(F32), 1).astype(BF16)
+        projected[rows, :] = contract_last(xn[rows, :], w_attn[...]).astype(BF16)
+        wide = matmul(projected[rows, :], key_value)
+        for which in range(2):
+            part = wide[:, WIDE * which : WIDE * (which + 1)] * own_in[...]
+            packed = jnp.sum(part.reshape(8, 32, WIDE), axis=0)
+            keyval_in[which * 2 + group] = packed.astype(BF16)
+    pl.semaphore_wait(barrier, 37)
+    mine = keyval.at[z_hi * 4 + x, core]
+    z_up, z_down, x_up, x_down = after(z_hi, 0, 4), after(z_hi, 2, 4), after(x, 0, 4), after(x, 2, 4)
+    push(keyval_in, mine, KV_Z_NEAR, {"z_hi": z_up})
+    push(keyval_in, mine, KV_Z_NEAR + 1, {"z_hi": z_down})
+    keep(keyval_in, mine, KV_Z_NEAR)
+
+    for copy in loads[2:]:
         copy.wait()
     mask_f = mask[...].astype(F32)
     lane = lax.broadcasted_iota(jnp.int32, (1024, 128), 1)
@@ -176,7 +208,6 @@
         normed[rows, :] = layer_norm(pair[rows, :].astype(F32), 1).astype(BF16)
         factor(block, 0)
     left_in[...] = rows_f[...].astype(BF16).reshape(16, 8, 16, 128)
-    pl.semaphore_wait(barrier, 37)
     for step in range(4):
         over_z(left_in, left_z, LEFT_QUARTER + step, step)
     for block in range(8):
@@ -184,36 +215,18 @@
     right_in[...] = rows_f[...].astype(BF16).reshape(16, 8, 16, 128)
     for step in range(4):
         over_x(right_in, right_x, RIGHT_X, step, quarter(step))
-    loads[3].wait()
     half_out = w_out.at[:, pl.ds(pl.multiple_of(core * 384, 128), 384)]
     each(3, lambda step: push(half_out, w_out_all.at[core, head], OUT_Z, near("z_lo", z_lo, step, 4)))
     keep(half_out, w_out_all.at[core, head], OUT_Z)
 
-    for copy in loads[4:]:
-        copy.wait()
-    lane = lax.broadcasted_iota(jnp.int32, (1, 4 * WIDE), 1)
-    block = block_of(lane)
-    source = lane - HEAD_DIM * block + HEAD_DIM * sum((block >= 8 * n).astype(jnp.int32) for n in (1, 2, 3))
-    place = lax.broadcasted_iota(jnp.int32, (4 * HEAD_DIM, 4 * WIDE), 0)
-    spread = (place == source).astype(F32).astype(BF16)
-    place = lax.broadcasted_iota(jnp.int32, (256, WIDE), 0)
-    own_block = ((place >= 32 * block[:, :WIDE]) & (place < 32 * block[:, :WIDE] + 32)).astype(F32)
     lane = lax.broadcasted_iota(jnp.int32, (WIDE, 128), 1)
     place = lax.broadcasted_iota(jnp.int32, (WIDE, 128), 0)
-    gather = (place - HEAD_DIM * block_of(place) == lane).astype(F32).astype(BF16)
-    own_in[...] = own_block
-    gather_in[...] = gather
-    w_wide = matmul(w_attn[...].T, spread).astype(BF16)
+    gather_in[...] = (place - HEAD_DIM * block_of(place) == lane).astype(F32).astype(BF16)
+    w_gate = matmul(w_attn[...].T, spread(3, 1)).astype(BF16)
     for group in range(2):
         rows = slice(group * 256, group * 256 + 256)
-        xn = layer_norm(single[rows, :].astype(F32), 1).astype(BF16)
-        wide = matmul(xn, w_wide)
-        query[rows, :] = (wide[:, 0:WIDE] * own_in[...]).astype(BF16)
-        for which in range(2):
-            part = wide[:, WIDE * (which + 1) : WIDE * (which + 2)] * own_in[...]
-            packed = jnp.sum(part.reshape(8, 32, WIDE), axis=0)
-            keyval_in[which * 2 + group] = packed.astype(BF16)
-        agate[rows, :] = jax.nn.sigmoid(wide[:, 3 * WIDE :])
+        query[rows, :] = (matmul(projected[rows, :], spread(0, 1)) * own_in[...]).astype(BF16)
+        agate[rows, :] = jax.nn.sigmoid(matmul(xn[rows, :], w_gate))
 
     def sent_z(slot, step):
         wait_bytes(left_z.at[pl.ds(0, 3 if step == 3 else 4)], send.at[slot + step])
@@ -222,11 +235,6 @@
         end_x(right_x, RIGHT_X, step)
         sent_z(LEFT_QUARTER, step)
         over_z(right_x, right_z, RIGHT_QUARTER + step, step)
-    mine = keyval.at[z_hi * 4 + x, core]
-    z_up, z_down, x_up, x_down = after(z_hi, 0, 4), after(z_hi, 2, 4), after(x, 0, 4), after(x, 2, 4)
-    push(keyval_in, mine, KV_Z_NEAR, {"z_hi": z_up})
-    push(keyval_in, mine, KV_Z_NEAR + 1, {"z_hi": z_down})
-    keep(keyval_in, mine, KV_Z_NEAR)
     wait_bytes(w_out_all.at[0, pl.ds(0, 1)], local.at[OUT_Z])
     wait_bytes(w_out_all.at[0, pl.ds(0, 3)], recv.at[OUT_Z])
     quad = w_out_all.at[core, pl.ds(y * 4, 4)]
@@ -463,6 +471,8 @@
         + [
             pltpu.VMEM((WIDE, 128), BF16),
             pltpu.VMEM((256, WIDE), F32),
+            pltpu.VMEM((512, 768), BF16),
+            pltpu.VMEM((512, 4 * HEAD_DIM), BF16),
             pltpu.VMEM((4, 4, 256, 256), BF16),
             pltpu.VMEM((4, 256, 256), BF16),
             pltpu.VMEM((16, 2, 4, 32, WIDE), BF16),

time: 133 us -> 138 us (1.038)
  Pallas kernels: 127 us -> 134 us
    pallas_call x1, Pallas kernels: 127 us -> 134 us  [per_device(): pl.pallas_call(whole_kernel, out_shape=(jax.ShapeDtypeStruct((2048, 128),...]
where the time goes in v9:
time: 138 us
  Pallas kernels  134 us (97%)
  local copies, waits for them, and re-layouts  3.33 us (2%)
    pallas_call x1, Pallas kernels, per_device(): pl.pallas_call(whole_kernel, out_shape=(jax.ShapeDtypeStruct((2048, 128),...  134 us
    unnamed x7, local copies, waits for them, and re-layouts  3.33 us

profile of v9, /device:TPU:6, one launch (start us, length us, event | category | flops | bytes accessed | tf_op | source)
XLA Modules:
  0.0 137.6 jit_solution(8404948431385525747)
XLA Ops:
  0.6 133.6 %whole.1 = (bf16[2048,128]{1,0:T(8,128)(2,1)}, bf16[4,32,1024]{2,1,0:T(8,128)(2,1)}, bf16[32,768]{1,0:T(8,128)(2,1)}) custom-call(bf16[2048,128]{1,0:T(8,128)(2,1)} %bitcast.14, s32[1,1024]{1,0:T(1,128)} %bitcast.19, bf16[128,640]{1,0:T(8,128)(2,1)} %w_tri_in_h.1, bf16[128,128]{1,0:T(8,128)(2,1)} %w_tri_out_h.1, bf16[64,128]{1,0:T(8,128)(2,1)} %bitcast.18, ...), custom_call_target="tpu_custom_call" | custom-call | tf_op jit(solution)/shard_map/whole/pallas_call | solution.py:451
  134.2 0.0 copy-start
  134.2 1.9 %copy.15 = bf16[32,64,128]{2,1,0:T(8,128)(2,1)} copy(bf16[32,64,128]{2,1,0:T(8,128)(2,1)} %bitcast.13) | data formatting | bytes 1048576
  136.2 0.0 copy-done
  136.2 0.0 copy-start.1
  136.2 0.7 copy.16
  136.9 0.1 copy-done.1
  137.0 0.6 copy.17
Async XLA Ops:
  134.2 1.9 %copy-start = (bf16[4,32,1024]{2,1,0:T(8,128)(2,1)S(1)}, bf16[4,32,1024]{2,1,0:T(8,128)(2,1)}, u32[]{:S(2)}) copy-start(bf16[4,32,1024]{2,1,0:T(8,128)(2,1)} %get-tuple-element.7) | copy-start | bytes 786436
  136.2 0.8 copy-start.1
